TPU v7x, 128 devices: a whole 4x4x4 slice. The times are simulated.
128 devices in a mesh: lon: 16 (over z, y_lo, core), lat: 8 (over y_hi, x).
Axes of the slice: x: 4, y: 4 (y_hi: 2, y_lo: 2; y = y_hi * 2 + y_lo), z: 4, core: 2. Of those that a mesh axis runs over, the one named last changes fastest.
Arguments:
- tokens: bfloat16 [2, 192, 576, 512], P(None, 'lat', 'lon'), may hold values from -16 to 16
- gain: float32 [512], replicated, may hold values from 0.1 to 1.9
- qkv_weight: bfloat16 [512, 1536], replicated, may hold values from -8 to 8
- out_weight: bfloat16 [512, 512], replicated, may hold values from -0.25 to 0.25
- cotangent: bfloat16 [2, 192, 576, 512], P(None, 'lat', 'lon'), may hold values from -6 to 6
Outputs:
- output: bfloat16 [2, 192, 576, 512], P(None, 'lat', 'lon')
- d_tokens: bfloat16 [2, 192, 576, 512], P(None, 'lat', 'lon')
- d_qkv_weight: float32 [512, 1536], P(('lon', 'lat'))
- d_out_weight: float32 [512, 512], P(('lon', 'lat'))
All inputs are finite; a program needn't handle non-finite values.
Results may differ from a plain program's by a relative error of at most 0.015.
The roundings to bfloat16 on the way count: a program that leaves them out, or rounds other values in their place, can miss the bound.
Values may be sent and summed in bfloat16 or wider, within the bound.
A program may use at most 128 MiB of HBM per device.

v0:
```python
import math

import jax
import jax.numpy as jnp
from jax import lax
from jax.sharding import PartitionSpec as P

HEAD = 32
WIN_LAT = 6
WIN_LON = 12


epsilon = 1e-05


def from_behind(block, axis, distance):
    devices = range(lax.axis_size(axis))
    route = [((i - distance) % len(devices), i) for i in devices]
    return lax.ppermute(block, axis, route)


def normalize(values_in):
    values = values_in.astype(jnp.float32)
    centre = values - jnp.mean(values, -1, keepdims=True)
    inverse = lax.rsqrt(jnp.mean(centre * centre, -1, keepdims=True) + epsilon)
    return (centre * inverse, inverse)


def take_lon(stacked, edge):
    return from_behind(stacked[:, :, :, :edge], "lon", -1)


def take_lat(stacked, edge):
    return from_behind(stacked[:, :, :edge], "lat", -1)


def give_lon(result, edge):
    return from_behind(result[:, :, -edge:], "lon", 1)


def give_lat(result, edge):
    return from_behind(result[:, -edge:], "lat", 1)


def extend(stacked, half_lat, half_lon):
    wider = jnp.concatenate([stacked[:, :, :, half_lon:], take_lon(stacked, half_lon)], 3)
    return jnp.concatenate([wider[:, :, half_lat:], take_lat(wider, half_lat)], 2)


def settle(result, half_lat, half_lon):
    placed = jnp.concatenate([give_lon(result, half_lon), result[:, :, :-half_lon]], 2)
    return jnp.concatenate([give_lat(placed, half_lat), placed[:, :-half_lat]], 1)


def attend(stacked, side_flag, qkv_weight):
    levels = stacked.shape[1]
    win_rows = stacked.shape[2]
    tile_cols = stacked.shape[3]
    model_width = stacked.shape[4]
    wide_count = tile_cols // WIN_LON
    window_len = levels * win_rows * WIN_LON
    head_count = model_width // HEAD
    score_scale = HEAD ** (-0.5)
    grouped = stacked.reshape(2, levels, win_rows, wide_count, WIN_LON, model_width)
    grouped = grouped.transpose(0, 3, 1, 2, 4, 5).reshape(2, wide_count, window_len, model_width)
    projected = jnp.einsum(
        "wtd,de->wte", grouped[0], qkv_weight, preferred_element_type=jnp.float32
    )
    projected = projected.astype(jnp.bfloat16).reshape(wide_count, window_len, 3, head_count, HEAD)
    query = projected[:, :, 0]
    key_part = projected[:, :, 1]
    value_part = projected[:, :, 2]
    d_attended = grouped[1].reshape(wide_count, window_len, head_count, HEAD)
    flags = jnp.broadcast_to(side_flag[None, :, None], (levels, win_rows, WIN_LON)).reshape(
        window_len
    )
    allowed = flags[:, None] == flags[None, :]
    scores = (
        jnp.einsum("wqhe,wkhe->whqk", query, key_part, preferred_element_type=jnp.float32)
        * score_scale
    )
    scores = jnp.where(allowed, scores, -1e30)
    peak = jnp.max(scores, -1, keepdims=True)
    expo = jnp.exp(scores - peak)
    weights = expo / jnp.sum(expo, -1, keepdims=True)
    weights_bf = weights.astype(jnp.bfloat16)
    attended = jnp.einsum(
        "whqk,wkhe->wqhe", weights_bf, value_part, preferred_element_type=jnp.float32
    ).astype(jnp.bfloat16)
    d_weights = jnp.einsum(
        "wqhe,wkhe->whqk", d_attended, value_part, preferred_element_type=jnp.float32
    )
    d_value = jnp.einsum(
        "whqk,wqhe->wkhe", weights_bf, d_attended, preferred_element_type=jnp.float32
    ).astype(jnp.bfloat16)
    d_scores = weights * (d_weights - jnp.sum(weights * d_weights, -1, keepdims=True)) * score_scale
    d_scores = d_scores.astype(jnp.bfloat16)
    d_query = jnp.einsum(
        "whqk,wkhe->wqhe", d_scores, key_part, preferred_element_type=jnp.float32
    ).astype(jnp.bfloat16)
    d_key = jnp.einsum(
        "whqk,wqhe->wkhe", d_scores, query, preferred_element_type=jnp.float32
    ).astype(jnp.bfloat16)
    joined = jnp.concatenate(
        [
            attended.reshape(wide_count, window_len, model_width),
            d_query.reshape(wide_count, window_len, model_width),
            d_key.reshape(wide_count, window_len, model_width),
            d_value.reshape(wide_count, window_len, model_width),
        ],
        -1,
    )
    joined = joined.reshape(wide_count, levels, win_rows, WIN_LON, 4 * model_width).transpose(
        1, 2, 0, 3, 4
    )
    return joined.reshape(levels, win_rows, tile_cols, 4 * model_width)


def per_device(tokens, gain, qkv_weight, out_weight, cotangent):
    levels, tile_rows, tile_cols, model_width = tokens.shape
    half_lat = WIN_LAT // 2
    half_lon = WIN_LON // 2
    devices = lax.axis_size("lon") * lax.axis_size("lat")
    grad_scale = 1.0 / math.sqrt(levels * tile_rows * tile_cols * devices)
    normed, inverse = normalize(tokens)
    hidden = (normed * gain).astype(jnp.bfloat16)
    d_attended = jnp.einsum(
        "lrce,de->lrcd", cotangent, out_weight, preferred_element_type=jnp.float32
    ).astype(jnp.bfloat16)
    stacked = jnp.stack([hidden, d_attended])
    region = extend(stacked, half_lat, half_lon)
    row_count = tile_rows // WIN_LAT
    slabs = region.reshape(2, levels, row_count, WIN_LAT, tile_cols, model_width).transpose(
        2, 0, 1, 3, 4, 5
    )
    top_device = lax.axis_index("lat") == lax.axis_size("lat") - 1
    row_ids = lax.broadcasted_iota(
        jnp.int32, (row_count, WIN_LAT), 0
    ) * WIN_LAT + lax.broadcasted_iota(jnp.int32, (row_count, WIN_LAT), 1)
    sides = jnp.logical_and(top_device, row_ids >= tile_rows - half_lat)
    pieces = lax.map(lambda inputs: attend(inputs[0], inputs[1], qkv_weight), (slabs, sides))
    result = pieces.transpose(1, 0, 2, 3, 4).reshape(levels, tile_rows, tile_cols, 4 * model_width)
    settled = settle(result, half_lat, half_lon)
    attended = settled[..., :model_width]
    d_projected = settled[..., model_width:]
    proj = jnp.einsum("lrcd,de->lrce", attended, out_weight, preferred_element_type=jnp.float32)
    output = (tokens.astype(jnp.float32) + proj).astype(jnp.bfloat16)
    d_hidden = jnp.einsum(
        "lrce,de->lrcd", d_projected, qkv_weight, preferred_element_type=jnp.float32
    )
    unit = d_hidden * gain
    d_tokens = cotangent.astype(jnp.float32) + inverse * (
        unit
        - jnp.mean(unit, -1, keepdims=True)
        - normed * jnp.mean(unit * normed, -1, keepdims=True)
    )
    d_tokens = d_tokens.astype(jnp.bfloat16)
    qkv_term = (
        jnp.einsum("lrcd,lrce->de", hidden, d_projected, preferred_element_type=jnp.float32)
        * grad_scale
    )
    out_term = (
        jnp.einsum("lrcd,lrce->de", attended, cotangent, preferred_element_type=jnp.float32)
        * grad_scale
    )
    d_qkv_weight, d_out_weight = (
        lax.psum_scatter(qkv_term, ("lon", "lat"), scatter_dimension=0, tiled=True),
        lax.psum_scatter(out_term, ("lon", "lat"), scatter_dimension=0, tiled=True),
    )
    return (output, d_tokens, d_qkv_weight, d_out_weight)


def solution(mesh):
    in_specs = (P(None, "lat", "lon", None), P(), P(), P(), P(None, "lat", "lon", None))
    out_specs = (
        P(None, "lat", "lon", None),
        P(None, "lat", "lon", None),
        P(("lon", "lat"), None),
        P(("lon", "lat"), None),
    )
    return jax.shard_map(
        per_device, mesh=mesh, in_specs=in_specs, out_specs=out_specs, check_vma=False
    )
```

profile of v0, /device:TPU:1, one launch (start us, length us, event | category | flops | bytes accessed | tf_op | source)
XLA Modules:
  0.0 643.4 jit_solution(4307884685922158598)
XLA Ops:
  20.1 6.6 %collective-permute-done = bf16[2,2,24,6,512]{4,2,3,1,0:T(8,128)(2,1)} collective-permute-done((bf16[2,2,24,6,512]{4,2,3,1,0:T(8,128)(2,1)S(1)}, bf16[2,2,24,6,512]{4,2,3,1,0:T(8,128)(2,1)}, u32[]{:S(2)}, u32[]{:S(2)}) %collective-permute-start) | collective-permute-done | bytes 589856 | tf_op jit(solution)/shard_map/ppermute | solution.py:19
  28.0 5.1 collective-permute-start.1
  34.2 6.6 %collective-permute-done.1 = bf16[2,2,3,36,512]{4,3,2,1,0:T(8,128)(2,1)S(1)} collective-permute-done((bf16[2,2,3,36,512]{4,3,2,1,0:T(8,128)(2,1)S(1)}, bf16[2,2,3,36,512]{4,3,2,1,0:T(8,128)(2,1)S(1)}, u32[]{:S(2)}, u32[]{:S(2)}) %collective-permute-start.1) | collective-permute-done | bytes 442400 | tf_op jit(solution)/shard_map/ppermute | solution.py:19
  41.1 5.4 copy.112
  46.5 368.3 %while.10 = (s32[]{:T(128)}, bf16[4,2,6,36,2048]{4,1,3,2,0:T(2,128)(2,1)}, bf16[4,2,2,6,36,512]{5,2,4,3,1,0:T(2,128)(2,1)}, bf16[512,1536]{1,0:T(8,128)(2,1)}, pred[4,6]{1,0:T(4,128)(4,1)S(1)}, /*index=5*/s32[]{:T(128)}) while((s32[]{:T(128)}, bf16[4,2,6,36,2048]{4,1,3,2,0:T(2,128)(2,1)}, bf16[4,2,2,6,36,512]{5,2,4,3,1,0:T(2,128)(2,1)}, ...), condition=%wide.region_6.7_spmd, body=%wide.region_2.6_spmd.sunk | while | flops 1094232192 | bytes 139345152 | solution.py:141
  52.5 3.3 convolution_convert_fusion.2
  58.4 4.0 fusion.118
  62.7 7.8 %fusion.119 = (f32[3,16,144]{2,1,0:T(8,128)S(1)}, f32[3,16,144,144]{2,3,1,0:T(8,128)S(1)}) fusion(f32[3,16,144,144]{2,3,1,0:T(8,128)} %fusion.118, pred[144,144]{0,1:T(8,128)(4,1)S(1)} %broadcast_compare_fusion.2), kind=kOutput, calls=%fused_computation.100.clone.1 | output fusion | flops 5972111 | bytes 8011008 | tf_op jit(solution)/shard_map/while/body/eval_jaxpr/sub | solution.py:84
  70.5 2.9 copy-done.22
  78.3 3.0 concatenate.32
  81.4 5.1 fusion.121
  86.5 11.3 %fusion.122 = bf16[3,144,16,32]{1,3,2,0:T(8,128)(2,1)} fusion(f32[3,16,144,144]{2,3,1,0:T(8,128)} %fusion.121, bf16[3,144,3,16,32]{1,4,3,2,0:T(8,128)(2,1)S(1)} %bitcast.127, f32[3,16,144,144]{2,3,1,0:T(8,128)} %copy-done.22, f32[3,16,144]{2,1,0:T(8,128)S(1)} %get-tuple-element.103), kind=kOutput, calls=%fused_computation.25.clone.1 | convolution fusion | flops 70896528 | bytes 29638656 | tf_op jit(solution)/shard_map/while/body/eval_jaxpr/whqk,wqhe->wkhe/dot_general | solution.py:101
  97.8 2.8 copy.127
  100.6 3.7 concatenate.33
  104.3 12.4 %fusion.123 = bf16[3,144,16,32]{1,3,2,0:T(8,128)(2,1)} fusion(f32[3,16,144,144]{2,3,1,0:T(8,128)} %fusion.121, bf16[3,144,3,16,32]{1,4,3,2,0:T(8,128)(2,1)S(1)} %bitcast.128, f32[3,16,144,144]{2,3,1,0:T(8,128)} %copy-done.22, f32[3,16,144]{2,1,0:T(8,128)S(1)} %get-tuple-element.103), kind=kOutput, calls=%fused_computation.26.clone.1 | convolution fusion | flops 70896528 | bytes 29638656 | tf_op jit(solution)/shard_map/while/body/eval_jaxpr/whqk,wkhe->wqhe/dot_general | solution.py:98
  119.5 3.8 concatenate.34
  123.2 4.5 fusion.124
  135.8 2.9 constant_dynamic-update-slice_fusion.2
  144.5 3.3 convolution_convert_fusion.2
  150.4 4.0 fusion.118
  154.7 7.8 %fusion.119 = (f32[3,16,144]{2,1,0:T(8,128)S(1)}, f32[3,16,144,144]{2,3,1,0:T(8,128)S(1)}) fusion(f32[3,16,144,144]{2,3,1,0:T(8,128)} %fusion.118, pred[144,144]{0,1:T(8,128)(4,1)S(1)} %broadcast_compare_fusion.2), kind=kOutput, calls=%fused_computation.100.clone.1 | output fusion | flops 5972111 | bytes 8011008 | tf_op jit(solution)/shard_map/while/body/eval_jaxpr/sub | solution.py:84
  162.5 2.9 copy-done.22
  167.5 2.8 copy.126
  170.3 3.0 concatenate.32
  173.3 5.1 fusion.121
  178.4 11.3 %fusion.122 = bf16[3,144,16,32]{1,3,2,0:T(8,128)(2,1)} fusion(f32[3,16,144,144]{2,3,1,0:T(8,128)} %fusion.121, bf16[3,144,3,16,32]{1,4,3,2,0:T(8,128)(2,1)S(1)} %bitcast.127, f32[3,16,144,144]{2,3,1,0:T(8,128)} %copy-done.22, f32[3,16,144]{2,1,0:T(8,128)S(1)} %get-tuple-element.103), kind=kOutput, calls=%fused_computation.25.clone.1 | convolution fusion | flops 70896528 | bytes 29638656 | tf_op jit(solution)/shard_map/while/body/eval_jaxpr/whqk,wqhe->wkhe/dot_general | solution.py:101
  189.8 2.8 copy.127
  192.5 3.7 concatenate.33
  196.3 12.4 %fusion.123 = bf16[3,144,16,32]{1,3,2,0:T(8,128)(2,1)} fusion(f32[3,16,144,144]{2,3,1,0:T(8,128)} %fusion.121, bf16[3,144,3,16,32]{1,4,3,2,0:T(8,128)(2,1)S(1)} %bitcast.128, f32[3,16,144,144]{2,3,1,0:T(8,128)} %copy-done.22, f32[3,16,144]{2,1,0:T(8,128)S(1)} %get-tuple-element.103), kind=kOutput, calls=%fused_computation.26.clone.1 | convolution fusion | flops 70896528 | bytes 29638656 | tf_op jit(solution)/shard_map/while/body/eval_jaxpr/whqk,wkhe->wqhe/dot_general | solution.py:98
  211.4 3.8 concatenate.34
  215.2 4.5 fusion.124
  227.8 2.8 constant_dynamic-update-slice_fusion.2
  236.4 3.3 convolution_convert_fusion.2
  242.3 4.0 fusion.118
  246.6 7.8 %fusion.119 = (f32[3,16,144]{2,1,0:T(8,128)S(1)}, f32[3,16,144,144]{2,3,1,0:T(8,128)S(1)}) fusion(f32[3,16,144,144]{2,3,1,0:T(8,128)} %fusion.118, pred[144,144]{0,1:T(8,128)(4,1)S(1)} %broadcast_compare_fusion.2), kind=kOutput, calls=%fused_computation.100.clone.1 | output fusion | flops 5972111 | bytes 8011008 | tf_op jit(solution)/shard_map/while/body/eval_jaxpr/sub | solution.py:84
  254.4 2.9 copy-done.22
  262.2 3.0 concatenate.32
  265.3 5.1 fusion.121
  270.4 11.3 %fusion.122 = bf16[3,144,16,32]{1,3,2,0:T(8,128)(2,1)} fusion(f32[3,16,144,144]{2,3,1,0:T(8,128)} %fusion.121, bf16[3,144,3,16,32]{1,4,3,2,0:T(8,128)(2,1)S(1)} %bitcast.127, f32[3,16,144,144]{2,3,1,0:T(8,128)} %copy-done.22, f32[3,16,144]{2,1,0:T(8,128)S(1)} %get-tuple-element.103), kind=kOutput, calls=%fused_computation.25.clone.1 | convolution fusion | flops 70896528 | bytes 29638656 | tf_op jit(solution)/shard_map/while/body/eval_jaxpr/whqk,wqhe->wkhe/dot_general | solution.py:101
  284.5 3.7 concatenate.33
  288.2 12.4 %fusion.123 = bf16[3,144,16,32]{1,3,2,0:T(8,128)(2,1)} fusion(f32[3,16,144,144]{2,3,1,0:T(8,128)} %fusion.121, bf16[3,144,3,16,32]{1,4,3,2,0:T(8,128)(2,1)S(1)} %bitcast.128, f32[3,16,144,144]{2,3,1,0:T(8,128)} %copy-done.22, f32[3,16,144]{2,1,0:T(8,128)S(1)} %get-tuple-element.103), kind=kOutput, calls=%fused_computation.26.clone.1 | convolution fusion | flops 70896528 | bytes 29638656 | tf_op jit(solution)/shard_map/while/body/eval_jaxpr/whqk,wkhe->wqhe/dot_general | solution.py:98
  303.4 3.8 concatenate.34
  307.1 4.5 fusion.124
  319.7 2.8 constant_dynamic-update-slice_fusion.2
  328.3 3.3 convolution_convert_fusion.2
  334.2 4.0 fusion.118
  338.5 7.8 %fusion.119 = (f32[3,16,144]{2,1,0:T(8,128)S(1)}, f32[3,16,144,144]{2,3,1,0:T(8,128)S(1)}) fusion(f32[3,16,144,144]{2,3,1,0:T(8,128)} %fusion.118, pred[144,144]{0,1:T(8,128)(4,1)S(1)} %broadcast_compare_fusion.2), kind=kOutput, calls=%fused_computation.100.clone.1 | output fusion | flops 5972111 | bytes 8011008 | tf_op jit(solution)/shard_map/while/body/eval_jaxpr/sub | solution.py:84
  346.4 2.9 copy-done.22
  354.1 3.0 concatenate.32
  357.2 5.1 fusion.121
  362.3 11.3 %fusion.122 = bf16[3,144,16,32]{1,3,2,0:T(8,128)(2,1)} fusion(f32[3,16,144,144]{2,3,1,0:T(8,128)} %fusion.121, bf16[3,144,3,16,32]{1,4,3,2,0:T(8,128)(2,1)S(1)} %bitcast.127, f32[3,16,144,144]{2,3,1,0:T(8,128)} %copy-done.22, f32[3,16,144]{2,1,0:T(8,128)S(1)} %get-tuple-element.103), kind=kOutput, calls=%fused_computation.25.clone.1 | convolution fusion | flops 70896528 | bytes 29638656 | tf_op jit(solution)/shard_map/while/body/eval_jaxpr/whqk,wqhe->wkhe/dot_general | solution.py:101
  376.4 3.7 concatenate.33
  380.1 12.4 %fusion.123 = bf16[3,144,16,32]{1,3,2,0:T(8,128)(2,1)} fusion(f32[3,16,144,144]{2,3,1,0:T(8,128)} %fusion.121, bf16[3,144,3,16,32]{1,4,3,2,0:T(8,128)(2,1)S(1)} %bitcast.128, f32[3,16,144,144]{2,3,1,0:T(8,128)} %copy-done.22, f32[3,16,144]{2,1,0:T(8,128)S(1)} %get-tuple-element.103), kind=kOutput, calls=%fused_computation.26.clone.1 | convolution fusion | flops 70896528 | bytes 29638656 | tf_op jit(solution)/shard_map/while/body/eval_jaxpr/whqk,wkhe->wqhe/dot_general | solution.py:98
  395.3 3.8 concatenate.34
  399.0 4.5 fusion.124
  411.6 2.8 constant_dynamic-update-slice_fusion.2
  414.8 6.5 %copy.73 = bf16[2,4,6,36,2048]{4,3,2,1,0:T(8,128)(2,1)S(1)} copy(bf16[2,4,6,36,2048]{4,0,3,2,1:T(2,128)(2,1)} %bitcast.140) | data formatting | bytes 14155776 | tf_op jit(solution)/shard_map/transpose | solution.py:142
  425.1 12.4 %collective-permute-done.2 = bf16[2,24,6,2048]{3,1,2,0:T(8,128)(2,1)S(1)} collective-permute-done((bf16[2,24,6,2048]{3,1,2,0:T(8,128)(2,1)S(1)}, bf16[2,24,6,2048]{3,1,2,0:T(8,128)(2,1)S(1)}, u32[]{:S(2)}, u32[]{:S(2)}) %collective-permute-start.2) | collective-permute-done | bytes 1179680 | tf_op jit(solution)/shard_map/ppermute | solution.py:19
  439.6 20.4 %collective-permute-done.3 = bf16[2,3,36,2048]{3,0,2,1:T(2,128)(2,1)} collective-permute-done((bf16[2,3,36,2048]{3,0,2,1:T(2,128)(2,1)S(1)}, bf16[2,3,36,2048]{3,0,2,1:T(2,128)(2,1)}, u32[]{:S(2)}, u32[]{:S(2)}) %collective-permute-start.3) | collective-permute-done | bytes 884768 | tf_op jit(solution)/shard_map/ppermute | solution.py:19
  464.8 5.8 fusion.66
  472.9 3.6 fusion.64
  479.1 4.7 multiply_reduce_fusion.1
  483.9 3.3 fusion.62
  489.0 144.7 %all-reduce.5.cloned.1.call-done = (f32[512,1536]{1,0:T(8,128)}, f32[512,512]{1,0:T(8,128)}) async-done(((f32[512,1536]{1,0:T(8,128)}, f32[512,512]{1,0:T(8,128)}), (f32[512,1536]{1,0:T(8,128)}, f32[512,512]{1,0:T(8,128)})) %all-reduce.5.cloned.1.call-update) | async-done | bytes 4194320
  (182 shorter events, 135.6 us)
Async XLA Ops:
  7.2 4.8 copy-start
  7.2 626.5 %all-reduce.5.cloned.1.call-start = ((), (), s32[]{:S(2)}) async-start(), calls=%async_computation | async-start | bytes 8388608
  9.3 5.4 copy-start.4
  9.4 5.4 copy-start.19
  9.4 6.3 copy-start.15
  12.0 3.7 copy-start.17
  14.8 1.3 copy-start.9
  16.3 10.4 %collective-permute-start = (bf16[2,2,24,6,512]{4,2,3,1,0:T(8,128)(2,1)S(1)}, bf16[2,2,24,6,512]{4,2,3,1,0:T(8,128)(2,1)}, u32[]{:S(2)}, u32[]{:S(2)}) collective-permute-start(bf16[2,2,24,6,512]{4,2,3,1,0:T(8,128)(2,1)S(1)} %copy.70), channel_id=1, source_target_pairs={{8,0},{16,8},{24,16},{32,24},{40,32},{48,40},{56,48},{64,56},{72,6... | collective-permute-start | bytes 1769480 | tf_op jit(solution)/shard_map/ppermute | solution.py:19
  28.0 12.7 %collective-permute-start.1 = (bf16[2,2,3,36,512]{4,3,2,1,0:T(8,128)(2,1)S(1)}, bf16[2,2,3,36,512]{4,3,2,1,0:T(8,128)(2,1)S(1)}, u32[]{:S(2)}, u32[]{:S(2)}) collective-permute-start(bf16[2,2,3,36,512]{4,3,2,1,0:T(8,128)(2,1)S(1)} %pad_maximum_fusion.8), channel_id=1, source_target_pairs={{1,0},{2,1},{3,2},{4,3},{5,4},{6,5},{7,6},{0,7},{9,8},{10,9},{11,1... | collective-permute-start | bytes 1327112 | tf_op jit(solution)/shard_map/ppermute | solution.py:19
  62.7 10.7 %copy-start.1 = (bf16[3,144,16,32]{1,3,2,0:T(8,128)(2,1)S(1)}, bf16[3,144,16,32]{1,3,2,0:T(8,128)(2,1)}, u32[]{:S(2)}) copy-start(bf16[3,144,16,32]{1,3,2,0:T(8,128)(2,1)} %copy.123) | copy-start | bytes 1327108 | tf_op jit(solution)/shard_map/while
  70.5 2.9 copy-start.22
  127.7 4.6 copy-start.2
  154.7 10.7 %copy-start.1 = (bf16[3,144,16,32]{1,3,2,0:T(8,128)(2,1)S(1)}, bf16[3,144,16,32]{1,3,2,0:T(8,128)(2,1)}, u32[]{:S(2)}) copy-start(bf16[3,144,16,32]{1,3,2,0:T(8,128)(2,1)} %copy.123) | copy-start | bytes 1327108 | tf_op jit(solution)/shard_map/while
  162.5 2.9 copy-start.22
  219.7 4.6 copy-start.2
  246.6 10.7 %copy-start.1 = (bf16[3,144,16,32]{1,3,2,0:T(8,128)(2,1)S(1)}, bf16[3,144,16,32]{1,3,2,0:T(8,128)(2,1)}, u32[]{:S(2)}) copy-start(bf16[3,144,16,32]{1,3,2,0:T(8,128)(2,1)} %copy.123) | copy-start | bytes 1327108 | tf_op jit(solution)/shard_map/while
  254.4 2.9 copy-start.22
  311.6 4.6 copy-start.2
  338.5 10.7 %copy-start.1 = (bf16[3,144,16,32]{1,3,2,0:T(8,128)(2,1)S(1)}, bf16[3,144,16,32]{1,3,2,0:T(8,128)(2,1)}, u32[]{:S(2)}) copy-start(bf16[3,144,16,32]{1,3,2,0:T(8,128)(2,1)} %copy.123) | copy-start | bytes 1327108 | tf_op jit(solution)/shard_map/while
  346.3 2.9 copy-start.22
  403.5 4.6 copy-start.2
  422.6 14.9 %collective-permute-start.2 = (bf16[2,24,6,2048]{3,1,2,0:T(8,128)(2,1)S(1)}, bf16[2,24,6,2048]{3,1,2,0:T(8,128)(2,1)S(1)}, u32[]{:S(2)}, u32[]{:S(2)}) collective-permute-start(bf16[2,24,6,2048]{3,1,2,0:T(8,128)(2,1)S(1)} %copy.74), channel_id=1, source_target_pairs={{120,0},{0,8},{8,16},{16,24},{24,32},{32,40},{40,48},{48,56},{56,6... | collective-permute-start | bytes 3538952 | tf_op jit(solution)/shard_map/ppermute | solution.py:19
  425.1 13.3 %copy-start.3 = (bf16[2,24,30,2048]{3,2,1,0:T(8,128)(2,1)}, bf16[2,24,30,2048]{3,2,1,0:T(8,128)(2,1)S(1)}, u32[]{:S(2)}) copy-start(bf16[2,24,30,2048]{3,2,1,0:T(8,128)(2,1)S(1)} %slice.67) | copy-start | bytes 17694724
  438.1 26.2 %copy-start.7 = (bf16[2,24,6,2048]{3,2,1,0:T(8,128)(2,1)}, bf16[2,24,6,2048]{3,2,1,0:T(8,128)(2,1)S(1)}, u32[]{:S(2)}) copy-start(bf16[2,24,6,2048]{3,2,1,0:T(8,128)(2,1)S(1)} %copy.75) | copy-start | bytes 3538948
  439.4 20.7 %collective-permute-start.3 = (bf16[2,3,36,2048]{3,0,2,1:T(2,128)(2,1)S(1)}, bf16[2,3,36,2048]{3,0,2,1:T(2,128)(2,1)}, u32[]{:S(2)}, u32[]{:S(2)}) collective-permute-start(bf16[2,3,36,2048]{3,0,2,1:T(2,128)(2,1)S(1)} %copy.76), channel_id=1, source_target_pairs={{7,0},{0,1},{1,2},{2,3},{3,4},{4,5},{5,6},{6,7},{15,8},{8,9},{9,10... | collective-permute-start | bytes 2654216 | tf_op jit(solution)/shard_map/ppermute | solution.py:19
  460.0 4.4 slice-start
  461.7 2.7 copy-start.10
  461.7 2.7 slice-start.1
  461.7 3.0 copy-start.5
  461.7 3.0 copy-start.16
  461.7 3.0 copy-start.18
  461.7 3.0 copy-start.20
  464.8 5.8 copy-start.12
  464.8 5.8 copy-start.13
  472.9 5.5 slice-start.2
  472.9 5.4 slice-start.3
  472.9 5.4 copy-start.6
  472.9 5.4 copy-start.8
  472.9 5.4 copy-start.11
  472.9 6.2 copy-start.21
  479.1 4.8 copy-start.14
Sparse Core Ops, SparseCore 0:
  473.0 160.6 all-reduce.4
where the time goes:
time: 653 us; the launch traced here: 643 us
  waiting for transfers between devices  191 us (29%)
  matrix products  190 us (29%)
  local copies, waits for them, and re-layouts  184 us (28%)
  other arithmetic  53.7 us (8%)
  between operations  14.7 us (2%)
  starting transfers between devices  8.61 us (1%)
    unnamed x2, waiting for transfers between devices  145 us
    concatenate x16, local copies, waits for them, and re-layouts, attend(): jnp.concatenate([attended.reshape(wide_count, window_len, model_width), d...  51.8 us
    dot_general x4, matrix products, attend(): jnp.einsum('whqk,wkhe->wqhe', d_scores, key_part, preferred_element_type=...  49.5 us
    ppermute x4, waiting for transfers between devices, from_behind(): return lax.ppermute(block, axis, route)  45.9 us
    dot_general x4, matrix products, attend(): jnp.einsum('whqk,wqhe->wkhe', d_scores, query, preferred_element_type=jnp...  45.3 us
    sub x4, other arithmetic, attend(): expo = jnp.exp(scores - peak)  31.2 us
    dot_general x4, matrix products, attend(): jnp.einsum('wqhe,wkhe->whqk', d_attended, value_part, preferred_element_t...  20.4 us
    dot_general x4, matrix products, attend(): jnp.einsum('whqk,wkhe->wqhe', weights_bf, value_part, preferred_element_t...  18.1 us
  transfers between devices with their start and end apart: 5, of which 5 were waited for; matrix products, arithmetic and copies ran while one was open for 3% of the time, Pallas kernels for 0%

commit v1 on v0

v1 whole, which is shorter than its diff:
```python
import functools
import math

import jax
import jax.numpy as jnp
import numpy as np
from jax import lax
from jax.experimental import pallas as pl
from jax.experimental.pallas import tpu as pltpu
from jax.sharding import PartitionSpec as P

F32, BF16 = jnp.float32, jnp.bfloat16
MESH = pl.DeviceIdType.MESH
D = 512
HEAD = 32
CELLS = 1728
WIN = 144
EPS = 1e-5
NN = (((1,), (0,)), ((), ()))
NT = (((1,), (1,)), ((), ()))
TN = (((0,), (0,)), ((), ()))
SCALE = HEAD**-0.5
SCALE_LOG2E = SCALE * math.log2(math.e)


def dot(a, b, dims=NN):
    return lax.dot_general(a, b, dims, preferred_element_type=F32)


def tables():
    order = np.zeros((192, 224), np.float32)
    place = np.zeros((192, 224), np.float32)
    squeeze = np.zeros((32, 192), np.float32)
    late = np.zeros((32, 48), np.float32)
    fill = np.zeros((144, 176), np.float32)
    for c in range(8):
        for rho in range(24):
            cell = (rho // 6) * 48 + c * 6 + rho % 6
            if rho < 21:
                order[cell, c * 24 + 3 + rho] = 1
                place[c * 24 + 3 + rho, cell] = 1
            else:
                order[cell, 192 + c * 4 + rho - 21] = 1
                place[c * 24 + rho - 21, 192 + c * 4 + rho - 21] = 1
                late[c * 4 + rho - 21, c * 6 + rho % 6] = 1
                squeeze[c * 4 + rho - 21, c * 24 + rho - 21] = 1
    for c in range(6):
        for row in range(24):
            fill[c * 24 + row, c * 24 + row if row >= 3 else 144 + 8 + c * 4 + row] = 1
    heads = np.zeros((128, 256), np.float32)
    for h in range(8):
        heads[16 * h : 16 * h + 16, 32 * h : 32 * h + 32] = 1
    bf = [jnp.asarray(t, BF16) for t in (order, place, squeeze, late, fill, heads)]
    return bf + [jnp.asarray(heads, F32)]


def groups(strip):
    c = 12 * strip
    return [[(0, c, 8)], [(0, c + 8, 4), (1, c, 4)], [(1, c + 4, 8)]]


def slot(strip, i):
    if strip < 2:
        return strip * 3 + i if i < 3 else 6 + strip
    return 8 + i


def attend(w, j, proj, datt, bias, hm, hmf, att, dproj, pt, st):
    rows = pl.ds(pl.multiple_of(w * WIN, 16), WIN)
    lo = 256 * j
    q = proj[rows, lo : lo + 256]
    k = proj[rows, 512 + lo : 768 + lo]
    v = proj[rows, 1024 + lo : 1280 + lo]
    da = datt[rows, lo : lo + 256]
    vt, kt = v.T, k.T

    def diagonal(x, c):
        if c == 4:
            return jnp.concatenate([x[128:144]] * 8, 0) * hm[...]
        one = [
            x[:128] * jnp.concatenate([hm[16 * h : 16 * h + 16, :]] * 8, 0)
            for h in (2 * c, 2 * c + 1)
        ]
        return jnp.concatenate(one, 0)

    qd = [diagonal(q, c) for c in range(5)]
    dd = [diagonal(da, c) for c in range(5)]
    am, qm = [], []
    for c in range(5):
        n = 256 if c < 4 else 128
        at = slice(256 * c, 256 * c + n)
        s = dot(k, qd[c], NT) + (bias[:, :256] if c < 4 else bias[:, 256:384])
        dw = dot(v, dd[c], NT)
        e = jnp.exp2((s - jnp.max(s, 0, keepdims=True)) * SCALE_LOG2E)
        p = e * (1.0 / jnp.sum(e, 0, keepdims=True))
        ds = p * (dw - jnp.sum(p * dw, 0, keepdims=True)) * SCALE
        p, ds = p.astype(BF16), ds.astype(BF16)
        pt[:, at] = p
        st[:, at] = ds
        if c < 4:
            a = dot(vt[64 * c : 64 * c + 64], p)
            am += [a[:32, :128], a[32:, 128:]]
            a = dot(kt[64 * c : 64 * c + 64], ds)
            qm += [a[:32, :128], a[32:, 128:]]
        else:
            a_end = (dot(p, v, TN) * hmf[...]).reshape(8, 16, 256).sum(0)
            q_end = (dot(ds, k, TN) * hmf[...]).reshape(8, 16, 256).sum(0)
    dv = dot(pt[...], jnp.concatenate(dd, 0))
    dk = dot(st[...], jnp.concatenate(qd, 0))
    join = lambda main, end: jnp.concatenate([jnp.concatenate(main, 0).T, end], 0).astype(BF16)
    att[rows, lo : lo + 256] = join(am, a_end)
    dproj[rows, lo : lo + 256] = join(qm, q_end)
    dproj[rows, 512 + lo : 768 + lo] = dk.astype(BF16)
    dproj[rows, 1024 + lo : 1280 + lo] = dv.astype(BF16)


def kernel(
    tok, cot, gain, wqkv, wo, order, place, squeeze, late, fill, hm, hmf,
    out, dtok, dqkv, dwo,
    own, edge, halo, corner, lsend, region, lout, lonin, latin, cornerin,
    tw, cw, hid, hidt, attt, inv, mean, proj, datt, att, dproj, bias, pt, st,
    gw, r0, s1a, r1a, s1b, r1b, s2a, r2a, s2b, r2b, s3, r3,
    local, send, recv,
):
    lon, lat = lax.axis_index("lon"), lax.axis_index("lat")
    lons, lats = lax.axis_size("lon"), lax.axis_size("lat")
    z, yl, core = lon // 4, (lon // 2) % 2, lon % 2
    yh, x = lat // 4, lat % 4
    west, east = (lon + lons - 1) % lons, (lon + 1) % lons
    south, north = (lat + lats - 1) % lats, (lat + 1) % lats
    dev = lambda a, b: {"lon": a, "lat": b}
    flip = lambda bit: 1 - bit
    twin = dev(z * 4 + yl * 2 + flip(core), lat)
    zs = [(z + d) % 4 for d in (1, 2, 3)]
    xs = [(x + d) % 4 for d in (1, 2, 3)]
    ys = [(flip(yl), yh), (yl, flip(yh)), (flip(yl), flip(yh))]
    zdev = [dev(a * 4 + yl * 2 + core, lat) for a in zs]
    ydev = [dev(z * 4 + a * 2 + core, b * 4 + x) for a, b in ys]
    xdev = [dev(lon, yh * 4 + a) for a in xs]

    loads = []
    for a, ref in enumerate((tok, cot)):
        loads.append(
            pltpu.make_async_copy(ref.at[:, 144:864], own.at[a, :, 0:720], local.at[2 * a])
        )
        loads.append(pltpu.make_async_copy(ref.at[:, 0:144], edge.at[a], local.at[2 * a + 1]))
    for copy in loads:
        copy.start()
    barrier = pltpu.get_barrier_semaphore()
    halo_devs = [dev(west, lat), dev(lon, south), dev(west, south)]
    halo_devs += [dev(east, lat), dev(lon, north), dev(east, north)]
    for target in halo_devs + [twin] + zdev + ydev + xdev:
        pl.semaphore_signal(barrier, inc=1, device_id=target, device_id_type=MESH)
    pl.semaphore_wait(barrier, 16)

    used = [0]

    def remote(src, dst, target):
        n = used[0]
        used[0] += 1
        return pltpu.make_async_remote_copy(
            src_ref=src,
            dst_ref=dst,
            send_sem=send.at[n],
            recv_sem=recv.at[n],
            device_id=target,
            device_id_type=MESH,
        )

    sends = []
    first = []
    for a, ref in enumerate((tok, cot)):
        first.append(remote(ref.at[:, 0:144], own.at[a, :, 720:864], dev(west, lat)))
        first[-1].start()
    latin[:, :, 128:144, :] = jnp.zeros((2, 2, 16, D), BF16)
    for copy in loads:
        copy.wait()

    def pairs_of(a, level, column, count):
        got = []
        here = min(count, max(0, 30 - column))
        if here:
            got.append(own[a, level, column * 24 : (column + here) * 24, :])
        if count - here:
            c = column + here - 30
            got.append(edge[a, level, c * 24 : (c + count - here) * 24, :])
        return got

    for a in range(2):
        for level in range(2):
            for column, count in ((0, 8), (8, 8), (16, 8), (24, 8), (32, 4)):
                cells = jnp.concatenate(pairs_of(a, level, column, count), 0)
                small = dot(squeeze[: count * 4, : count * 24], cells).astype(BF16)
                lsend[a, level, column * 4 : (column + count) * 4, :] = small
        first.append(remote(lsend.at[a, :, 0:128], halo.at[a, :, 0:128], dev(lon, south)))
        first.append(remote(lsend.at[a, :, 112:144], corner.at[a], dev(west, south)))
        first[-2].start()
        first[-1].start()

    def gather(a, strip, g, which):
        runs = groups(strip)[g]
        cells = [own[a, lev, c * 24 : (c + n) * 24, :] for lev, c, n in runs]
        lo, hi = which
        width = 192
        if hi == 4:
            cells += [halo[a, lev, c * 4 : (c + n) * 4, :] for lev, c, n in runs]
            width = 224
        got = dot(order[48 * lo : 48 * hi, :width], jnp.concatenate(cells, 0)).astype(BF16)
        for i in range(lo, hi):
            at = slot(strip, i) * WIN + g * 48
            (tw, cw)[a][at : at + 48, :] = got[(i - lo) * 48 : (i - lo) * 48 + 48]

    @pl.loop(0, 2)
    def _(part):
        @pl.when(part == 0)
        def _():
            for a in range(2):
                for strip in range(2):
                    for g in range(3):
                        gather(a, strip, g, (0, 3))

        @pl.when(part == 1)
        def _():
            for copy in first:
                copy.wait()
            late_row = lax.broadcasted_iota(jnp.int32, (32, D), 0) >= 8
            for a in range(2):
                for level in range(2):
                    halo[a, level, 112:144, :] = jnp.where(
                        late_row, corner[a, level], halo[a, level, 112:144, :]
                    )
                for g in range(3):
                    for strip in range(2):
                        gather(a, strip, g, (3, 4))
                    gather(a, 2, g, (0, 4))

        @pl.loop(0, 3)
        def _(t):
            rows = pl.ds(pl.multiple_of(part * 864 + t * 288, 16), 288)
            cells = tw[rows, :].astype(F32)
            mu = jnp.mean(cells, -1, keepdims=True)
            cells = cells - mu
            iv = lax.rsqrt(jnp.mean(cells * cells, -1, keepdims=True) + EPS)
            h = (cells * iv * gain[...]).astype(BF16)
            hid[rows, :] = h
            mean[rows, :] = mu
            inv[rows, :] = iv
            for n in range(3):
                at = slice(512 * n, 512 * n + 512)
                proj[rows, at] = dot(h, wqkv[:, at]).astype(BF16)
            datt[rows, :] = dot(cw[rows, :], wo[...], NT).astype(BF16)

        @pl.loop(part * 6, part * 6 + 6)
        def _(w):
            key_side = (lax.broadcasted_iota(jnp.int32, (WIN, 1), 0) % 6) >= 3
            lane = lax.broadcasted_iota(jnp.int32, (1, 384), 1)
            query = jnp.where(lane < 256, lane % 128, 128 + lane % 16)
            query_side = (query % 6) >= 3
            last = jnp.logical_or(jnp.logical_or(w == 6, w == 7), w == 11)
            apart = jnp.logical_and(last, lat == lats - 1)
            bias[...] = jnp.where(jnp.logical_and(apart, key_side != query_side), -1e30, 0.0)
            for j in range(2):
                attend(w, j, proj, datt, bias, hm, hmf, att, dproj, pt, st)

    grad_scale = 1.0 / math.sqrt(CELLS * 128)
    hidt[...] = hid[...].T
    attt[...] = att[...].T
    cores = []
    for half in range(2):
        for n in range(4 * half, 4 * half + 4):
            lo = 256 * n
            if n < 6:
                grad = dot(hidt[...], dproj[:, lo : lo + 256])
            else:
                grad = dot(attt[...], cw[:, lo - 1536 : lo - 1280])
            gw[:, :, :, lo : lo + 256] = (grad * grad_scale).reshape(8, 2, 32, 256)
        cols = slice(1024 * half, 1024 * half + 1024)
        cores.append(remote(gw.at[:, flip(core), :, cols], r0.at[:, :, cols], twin))
        cores[-1].start()

    res = (hid, datt)

    def outputs(w):
        rows = pl.ds(pl.multiple_of(w * WIN, 16), WIN)
        cells = tw[rows, :].astype(F32)
        res[0][rows, :] = (cells + dot(att[rows, :], wo[...])).astype(BF16)
        u = dot(dproj[rows, :], wqkv[...], NT) * gain[...]
        iv = inv[rows, :]
        normed = (cells - mean[rows, :]) * iv
        d = u - jnp.mean(u, -1, keepdims=True) - normed * jnp.mean(u * normed, -1, keepdims=True)
        res[1][rows, :] = (cw[rows, :].astype(F32) + iv * d).astype(BF16)

    def windows_of(a, strip, g):
        at = [slot(strip, i) * WIN + g * 48 for i in range(4)]
        return [res[a][n : n + 48, :] for n in at]

    pl.loop(6, 12)(outputs)

    for a in range(2):
        for strip in range(3):
            for g, runs in enumerate(groups(strip)):
                cells = windows_of(a, strip, g)
                small = dot(late[...], cells[3]).astype(BF16)
                at = 0
                for lev, c, n in runs:
                    lout[a, lev, c * 4 : (c + n) * 4, :] = small[at * 4 : (at + n) * 4]
                    at += n
                if strip == 2:
                    whole = dot(place[:, :192], jnp.concatenate(cells, 0)).astype(BF16)
                    at = 0
                    for lev, c, n in runs:
                        region[a, lev, c * 24 : (c + n) * 24, :] = whole[at * 24 : (at + n) * 24]
                        at += n
        sends.append(remote(region.at[a, :, 720:864], lonin.at[a], dev(east, lat)))
        sends.append(remote(lout.at[a, :, 0:128], latin.at[a, :, 0:128], dev(lon, north)))
        sends.append(remote(lout.at[a, :, 112:144], cornerin.at[a], dev(east, north)))
        for copy in sends[-3:]:
            copy.start()

    cores[0].wait()
    stage1 = []
    for k in range(8):
        total = gw[k, core, :, 0:1024] + r0[k, :, 0:1024]
        gw[k, core, :, 0:1024] = total
        s1a[k // 2, k % 2] = total.astype(BF16)
    for d in range(3):
        stage1.append(remote(s1a.at[zs[d]], r1a.at[d], zdev[d]))
        stage1[-1].start()
    cores[1].wait()
    for k in range(8):
        total = gw[k, core, :, 1024:2048] + r0[k, :, 1024:2048]
        gw[k, core, :, 1024:2048] = total
        low = total.astype(BF16)
        for h in range(2):
            s1b[k % 2, h, k // 2] = low[16 * h : 16 * h + 16]
    for d in range(3):
        stage1.append(remote(s1b.at[ys[d][0], ys[d][1]], r1b.at[d], ydev[d]))
        stage1[-1].start()

    pl.loop(0, 6)(outputs)

    stage2 = []
    for copy in stage1[:3]:
        copy.wait()
    for k in range(2):
        total = gw[z * 2 + k, core, :, 0:1024]
        for d in range(3):
            total = total + r1a[d, k].astype(F32)
        for h in range(2):
            s2a[k, h] = total[16 * h : 16 * h + 16]
    for d in range(3):
        stage2.append(remote(s2a.at[ys[d][0], ys[d][1]], r2a.at[d], ydev[d]))
        stage2[-1].start()
    for copy in stage1[3:]:
        copy.wait()
    for k in range(4):
        mine = pl.ds(pl.multiple_of(yh * 16, 16), 16)
        total = gw[k * 2 + yl, core, mine, 1024:2048]
        for d in range(3):
            total = total + r1b[d, k].astype(F32)
        s2b[k] = total
    for d in range(3):
        stage2.append(remote(s2b.at[zs[d]], r2b.at[d], zdev[d]))
        stage2[-1].start()

    for copy in sends:
        copy.wait()
    for a in range(2):
        for level in range(2):
            edge_in = jnp.concatenate([lonin[a, level], cornerin[a, level]], 0)
            edge[a, level] = dot(fill[...], edge_in).astype(BF16)
        for strip in range(3):
            for g, runs in enumerate(groups(strip)):
                cells = windows_of(a, strip, g)
                cells += [latin[a, lev, c * 4 : (c + n) * 4, :] for lev, c, n in runs]
                whole = dot(place[...], jnp.concatenate(cells, 0)).astype(BF16)
                at = 0
                for lev, c, n in runs:
                    keep = min(n, max(0, 30 - c))
                    if keep:
                        own[a, lev, c * 24 : (c + keep) * 24, :] = whole[at * 24 : (at + keep) * 24]
                    at += n
    stores = []
    for a, ref in enumerate((out, dtok)):
        stores.append(
            pltpu.make_async_copy(own.at[a, :, 0:720], ref.at[:, 144:864], local.at[2 * a])
        )
        stores.append(pltpu.make_async_copy(edge.at[a], ref.at[:, 0:144], local.at[2 * a + 1]))
    for copy in stores:
        copy.start()

    for copy in stage2:
        copy.wait()
    left = s2a[yl, yh]
    right = s2b[z]
    for d in range(3):
        left = left + r2a[d]
        right = right + r2b[d]
    for k in range(4):
        s3[k, 0:4, :] = left[4 * k : 4 * k + 4]
        s3[k, 4:8, :] = right[4 * k : 4 * k + 4]
    stage3 = []
    for d in range(3):
        stage3.append(remote(s3.at[xs[d]], r3.at[d], xdev[d]))
        stage3[-1].start()
    for copy in stage3:
        copy.wait()
    total = s3[x] + r3[0] + r3[1] + r3[2]
    dqkv[:, 0:1024] = total[0:4]
    dqkv[:, 1024:1536] = total[4:8, 0:512]
    dwo[...] = total[4:8, 512:1024]
    for copy in stores:
        copy.wait()


def per_device(tokens, gain, qkv_weight, out_weight, cotangent):
    by_column = lambda a: a.transpose(0, 2, 1, 3).reshape(2, 864, D)
    vmem = pl.BlockSpec(memory_space=pltpu.VMEM)
    hbm = pl.BlockSpec(memory_space=pl.ANY)
    shape = jax.ShapeDtypeStruct
    buf = lambda *dims: pltpu.VMEM(dims, BF16)
    buf32 = lambda *dims: pltpu.VMEM(dims, F32)
    consts = tables()
    copies = 6 + 2 + 6 + 6 + 6 + 3
    out, dtok, dqkv, dwo = pl.pallas_call(
        kernel,
        out_shape=(
            shape((2, 864, D), BF16),
            shape((2, 864, D), BF16),
            shape((4, 3 * D), F32),
            shape((4, D), F32),
        ),
        in_specs=[hbm, hbm] + [vmem] * (3 + len(consts)),
        out_specs=(hbm, hbm, vmem, vmem),
        scratch_shapes=[
            buf(2, 2, 864, D),
            buf(2, 2, 144, D),
            buf(2, 2, 144, D),
            buf(2, 2, 32, D),
            buf(2, 2, 144, D),
            buf(2, 2, 864, D),
            buf(2, 2, 144, D),
            buf(2, 2, 144, D),
            buf(2, 2, 144, D),
            buf(2, 2, 32, D),
            buf(CELLS, D),
            buf(CELLS, D),
            buf(CELLS, D),
            buf(D, CELLS),
            buf(D, CELLS),
            buf32(CELLS, 1),
            buf32(CELLS, 1),
            buf(CELLS, 3 * D),
            buf(CELLS, D),
            buf(CELLS, D),
            buf(CELLS, 3 * D),
            buf32(WIN, 384),
            buf(WIN, 1152),
            buf(WIN, 1152),
            buf32(8, 2, 32, 2048),
            buf32(8, 32, 2048),
            buf(4, 2, 32, 1024),
            buf(3, 2, 32, 1024),
            buf(2, 2, 4, 16, 1024),
            buf(3, 4, 16, 1024),
            buf32(2, 2, 16, 1024),
            buf32(3, 16, 1024),
            buf32(4, 16, 1024),
            buf32(3, 16, 1024),
            buf32(4, 8, 1024),
            buf32(3, 8, 1024),
            pltpu.SemaphoreType.DMA((4,)),
            pltpu.SemaphoreType.DMA((copies,)),
            pltpu.SemaphoreType.DMA((copies,)),
        ],
        compiler_params=pltpu.CompilerParams(
            collective_id=0, has_side_effects=True, vmem_limit_bytes=60 * 2**20
        ),
        name="block",
    )(
        by_column(tokens),
        by_column(cotangent),
        gain.reshape(1, D),
        qkv_weight,
        out_weight,
        *consts,
    )
    in_place = lambda a: a.reshape(2, 36, 24, D).transpose(0, 2, 1, 3)
    return in_place(out), in_place(dtok), dqkv, dwo


def solution(mesh):
    in_specs = (P(None, "lat", "lon", None), P(), P(), P(), P(None, "lat", "lon", None))
    out_specs = (
        P(None, "lat", "lon", None),
        P(None, "lat", "lon", None),
        P(("lon", "lat"), None),
        P(("lon", "lat"), None),
    )
    return jax.shard_map(
        per_device, mesh=mesh, in_specs=in_specs, out_specs=out_specs, check_vma=False
    )
```

time: 653 us -> 113 us (0.17); the launches traced: 643 us -> 113 us
  waiting for transfers between devices: 191 us -> 0 us
  matrix products: 190 us -> 0 us
  local copies, waits for them, and re-layouts: 184 us -> 5.36 us
  Pallas kernels: 0 us -> 107 us
  other arithmetic: 53.7 us -> 0 us
  between operations: 14.7 us -> 0.65 us
  starting transfers between devices: 8.61 us -> 0 us
    dot_general x33 -> x0, matrix products: 190 us -> none  [the longest x4 49.5 us: attend(): jnp.einsum('whqk,wkhe->wqhe', d_scores, key_part, preferred_element_type=...]
    unnamed x2 -> x0, waiting for transfers between devices: 145 us -> none
    pallas_call x0 -> x1, Pallas kernels: none -> 107 us  [per_device(): pl.pallas_call(kernel, out_shape=(shape((2, 864, D), BF16), shape((2, 864...]
    convert_element_type x20 -> x0, local copies, waits for them, and re-layouts: 52.4 us -> none  [the longest x4 11.1 us: attend(): d_key = jnp.einsum('whqk,wqhe->wkhe', d_scores, query, preferred_element_...]
    concatenate x16 -> x0, local copies, waits for them, and re-layouts: 51.8 us -> none  [attend(): jnp.concatenate([attended.reshape(wide_count, window_len, model_width), d...]
    ppermute x4 -> x0, waiting for transfers between devices: 45.9 us -> none  [from_behind(): return lax.ppermute(block, axis, route)]
    sub x4 -> x0, other arithmetic: 31.2 us -> none  [attend(): expo = jnp.exp(scores - peak)]
    transpose x5 -> x0, local copies, waits for them, and re-layouts: 13.9 us -> none  [the longest x4 7.37 us: attend(): joined.reshape(wide_count, levels, win_rows, WIN_LON, 4 * model_width)]
  transfers between devices with their start and end apart: 5 -> 0, of which waited for: 5 -> 0; matrix products, arithmetic and copies ran while one was open for 3% -> 0% of each run, Pallas kernels for 0% -> 0%
where the time goes in v1:
time: 113 us
  Pallas kernels  107 us (95%)
  local copies, waits for them, and re-layouts  5.36 us (5%)
    pallas_call x1, Pallas kernels, per_device(): pl.pallas_call(kernel, out_shape=(shape((2, 864, D), BF16), shape((2, 864...  107 us
    unnamed x10, local copies, waits for them, and re-layouts  5.36 us

profile of v1, /device:TPU:1, one launch (start us, length us, event | category | flops | bytes accessed | tf_op | source)
XLA Modules:
  0.0 112.9 jit_solution(7460716612501127449)
XLA Ops:
  0.6 106.9 %block.1 = (bf16[2,864,512]{2,1,0:T(8,128)(2,1)}, bf16[2,864,512]{2,1,0:T(8,128)(2,1)}, f32[4,1536]{1,0:T(4,128)}, f32[4,512]{1,0:T(4,128)}) custom-call(bf16[2,864,512]{2,1,0:T(8,128)(2,1)} %bitcast.13, bf16[2,864,512]{2,1,0:T(8,128)(2,1)} %bitcast.14, f32[1,512]{1,0:T(1,128)} %bitcast.17, bf16[512,1536]{1,0:T(8,128)(2,1)} %wqkv.1, bf16[512,512]{1,0:T(8,128)(2,1)} %wo.1, ...), custom_call_target="tpu_custom_call" | custom-call | tf_op jit(solution)/shard_map/block/pallas_call | solution.py:425
  107.6 0.0 copy-start
  107.6 2.9 %copy.20 = bf16[2,24,36,512]{3,1,2,0:T(8,128)(2,1)} copy(bf16[2,24,36,512]{3,1,2,0:T(8,128)(2,1)} %bitcast.16) | data formatting | bytes 3538944
  110.5 0.0 copy-done
  110.5 0.0 copy-start.1
  110.5 0.0 copy-start.2
  110.5 1.2 %copy.21 = bf16[2,24,36,512]{3,1,2,0:T(8,128)(2,1)} copy(bf16[2,24,36,512]{3,1,2,0:T(8,128)(2,1)S(1)} %bitcast.15) | data formatting | bytes 3538944
  111.7 0.0 copy-done.1
  111.7 0.6 copy.22
  112.3 0.0 copy-done.2
  112.3 0.6 copy.23
Async XLA Ops:
  107.6 2.9 %copy-start = (bf16[2,864,512]{2,1,0:T(8,128)(2,1)S(1)}, bf16[2,864,512]{2,1,0:T(8,128)(2,1)}, u32[]{:S(2)}) copy-start(bf16[2,864,512]{2,1,0:T(8,128)(2,1)} %get-tuple-element.9) | copy-start | bytes 5308420
  110.5 1.2 %copy-start.1 = (f32[4,1536]{1,0:T(4,128)S(1)}, f32[4,1536]{1,0:T(4,128)}, u32[]{:S(2)}) copy-start(f32[4,1536]{1,0:T(4,128)} %get-tuple-element.18) | copy-start | bytes 73732
  110.5 1.8 %copy-start.2 = (f32[4,512]{1,0:T(4,128)S(1)}, f32[4,512]{1,0:T(4,128)}, u32[]{:S(2)}) copy-start(f32[4,512]{1,0:T(4,128)} %get-tuple-element.19) | copy-start | bytes 24580

commit v2 on v1

v2 whole, which is shorter than its diff:
```python
import functools
import math

import jax
import jax.numpy as jnp
import numpy as np
from jax import lax
from jax.experimental import pallas as pl
from jax.experimental.pallas import tpu as pltpu
from jax.sharding import PartitionSpec as P

F32, BF16 = jnp.float32, jnp.bfloat16
MESH = pl.DeviceIdType.MESH
D = 512
HEAD = 32
CELLS = 1728
WIN = 144
EPS = 1e-5
NN = (((1,), (0,)), ((), ()))
NT = (((1,), (1,)), ((), ()))
TN = (((0,), (0,)), ((), ()))
SCALE = HEAD**-0.5
SCALE_LOG2E = SCALE * math.log2(math.e)


def dot(a, b, dims=NN):
    return lax.dot_general(a, b, dims, preferred_element_type=F32)


def tables():
    order = np.zeros((192, 224), np.float32)
    place = np.zeros((192, 224), np.float32)
    squeeze = np.zeros((32, 192), np.float32)
    late = np.zeros((32, 48), np.float32)
    fill = np.zeros((144, 176), np.float32)
    for c in range(8):
        for rho in range(24):
            cell = (rho // 6) * 48 + c * 6 + rho % 6
            if rho < 21:
                order[cell, c * 24 + 3 + rho] = 1
                place[c * 24 + 3 + rho, cell] = 1
            else:
                order[cell, 192 + c * 4 + rho - 21] = 1
                place[c * 24 + rho - 21, 192 + c * 4 + rho - 21] = 1
                late[c * 4 + rho - 21, c * 6 + rho % 6] = 1
                squeeze[c * 4 + rho - 21, c * 24 + rho - 21] = 1
    for c in range(6):
        for row in range(24):
            fill[c * 24 + row, c * 24 + row if row >= 3 else 144 + 8 + c * 4 + row] = 1
    heads = np.zeros((128, 256), np.float32)
    for h in range(8):
        heads[16 * h : 16 * h + 16, 32 * h : 32 * h + 32] = 1
    bf = [jnp.asarray(t, BF16) for t in (order, place, squeeze, late, fill, heads)]
    return bf + [jnp.asarray(heads, F32)]


def groups(strip):
    c = 12 * strip
    return [[(0, c, 8)], [(0, c + 8, 4), (1, c, 4)], [(1, c + 4, 8)]]


def slot(strip, i):
    if strip < 2:
        return strip * 3 + i if i < 3 else 6 + strip
    return 8 + i


def masked_tail(x, hm):
    return jnp.concatenate([x[128:144]] * 8, 0) * hm[...]


def diagonal(ref, x, hm):
    for h in range(8):
        at = slice(128 * (h // 4), 128 * (h // 4) + 128)
        mask = jnp.concatenate([hm[16 * h : 16 * h + 16, at]] * 8, 0)
        ref[128 * h : 128 * h + 128, at] = x[:128, at] * mask
    ref[1024:1152, :] = masked_tail(x, hm)


def diagonal_t(ref, x, hm):
    turned = x[:128].T
    for h in range(8):
        ref[32 * h : 32 * h + 32, 128 * h : 128 * h + 128] = turned[32 * h : 32 * h + 32]
    ref[:, 1024:1152] = masked_tail(x, hm).T


def by_query(dst, src):
    for h in range(8):
        at = slice(128 * h, 128 * h + 128)
        dst[:, at] = src[0:128, at].T
    ends = [src[128:144, 128 * h : 128 * h + 128] for h in range(8)]
    dst[:, 1024:1152] = jnp.concatenate(ends, 0).T


def last_queries(src, x, hmf):
    each = dot(src[:, 1024:1152], x, TN) * hmf[...]
    return each.reshape(8, 16, 256).sum(0)


def attend(w, lo, proj, datt, bias, hm, hmf, att, dproj, bufs):
    qt, dt, sc, dw, pt, gt, pq, gq, qd, dd, kd, vd = bufs
    rows = pl.ds(pl.multiple_of(w * WIN, 16), WIN)
    cols = lambda off: pl.ds(pl.multiple_of(off + lo, 256), 256)
    q, k, v = proj[rows, cols(0)], proj[rows, cols(512)], proj[rows, cols(1024)]
    da = datt[rows, cols(0)]
    diagonal_t(qt, q, hm)
    diagonal_t(dt, da, hm)
    sc[...] = dot(k, qt[...])
    dw[...] = dot(v, dt[...])
    for c in range(9):
        at = slice(128 * c, 128 * c + 128)
        s = sc[:, at] + (bias[:, :128] if c < 8 else bias[:, 128:256])
        d = dw[:, at]
        e = jnp.exp2((s - jnp.max(s, 0, keepdims=True)) * SCALE_LOG2E)
        p = e * (1.0 / jnp.sum(e, 0, keepdims=True))
        pt[:, at] = p.astype(BF16)
        gt[:, at] = (p * (d - jnp.sum(p * d, 0, keepdims=True)) * SCALE).astype(BF16)
    diagonal(dd, da, hm)
    dproj[rows, cols(1024)] = dot(pt[...], dd[...]).astype(BF16)
    by_query(pq, pt)
    diagonal(vd, v, hm)
    a = jnp.concatenate([dot(pq[...], vd[...]), last_queries(pt, v, hmf)], 0)
    att[rows, cols(0)] = a.astype(BF16)
    diagonal(qd, q, hm)
    dproj[rows, cols(512)] = dot(gt[...], qd[...]).astype(BF16)
    by_query(gq, gt)
    diagonal(kd, k, hm)
    dq = jnp.concatenate([dot(gq[...], kd[...]), last_queries(gt, k, hmf)], 0)
    dproj[rows, cols(0)] = dq.astype(BF16)


def kernel(
    tok, cot, gain, wqkv, wo, order, place, squeeze, late, fill, hm, hmf,
    out, dtok, dqkv, dwo,
    own, edge, halo, corner, lsend, region, lout, lonin, latin, cornerin,
    tw, cw, hid, hidt, attt, inv, mean, proj, datt, att, dproj, bias, *more,
):
    bufs, more = more[:12], more[12:]
    sums = (more[:12], more[12:24])
    local, send, recv = more[24:]
    lon, lat = lax.axis_index("lon"), lax.axis_index("lat")
    lons, lats = lax.axis_size("lon"), lax.axis_size("lat")
    z, yl, core = lon // 4, (lon // 2) % 2, lon % 2
    yh, x = lat // 4, lat % 4
    west, east = (lon + lons - 1) % lons, (lon + 1) % lons
    south, north = (lat + lats - 1) % lats, (lat + 1) % lats
    dev = lambda a, b: {"lon": a, "lat": b}
    flip = lambda bit: 1 - bit
    twin = dev(z * 4 + yl * 2 + flip(core), lat)
    zs = [(z + d) % 4 for d in (1, 2, 3)]
    xs = [(x + d) % 4 for d in (1, 2, 3)]
    ys = [(flip(yl), yh), (yl, flip(yh)), (flip(yl), flip(yh))]
    zdev = [dev(a * 4 + yl * 2 + core, lat) for a in zs]
    ydev = [dev(z * 4 + a * 2 + core, b * 4 + x) for a, b in ys]
    xdev = [dev(lon, yh * 4 + a) for a in xs]

    loads = []
    for a, ref in enumerate((tok, cot)):
        loads.append(
            pltpu.make_async_copy(ref.at[:, 144:864], own.at[a, :, 0:720], local.at[2 * a])
        )
        loads.append(pltpu.make_async_copy(ref.at[:, 0:144], edge.at[a], local.at[2 * a + 1]))
    for copy in loads:
        copy.start()
    barrier = pltpu.get_barrier_semaphore()
    halo_devs = [dev(west, lat), dev(lon, south), dev(west, south)]
    halo_devs += [dev(east, lat), dev(lon, north), dev(east, north)]
    for target in halo_devs + [twin] + zdev + ydev + xdev:
        pl.semaphore_signal(barrier, inc=1, device_id=target, device_id_type=MESH)

    used = [0]

    def remote(src, dst, target):
        n = used[0]
        used[0] += 1
        return pltpu.make_async_remote_copy(
            src_ref=src,
            dst_ref=dst,
            send_sem=send.at[n],
            recv_sem=recv.at[n],
            device_id=target,
            device_id_type=MESH,
        )

    halo_in, halo_out = [], []
    for a, ref in enumerate((tok, cot)):
        halo_in.append(remote(ref.at[:, 0:144], own.at[a, :, 720:864], dev(west, lat)))
        halo_in.append(remote(lsend.at[a, :, 0:128], halo.at[a, :, 0:128], dev(lon, south)))
        halo_in.append(remote(lsend.at[a, :, 112:144], corner.at[a], dev(west, south)))
        halo_out.append(remote(region.at[a, :, 144:288], lonin.at[a], dev(east, lat)))
        halo_out.append(remote(lout.at[a, :, 0:128], latin.at[a, :, 0:128], dev(lon, north)))
        halo_out.append(remote(lout.at[a, :, 112:144], cornerin.at[a], dev(east, north)))

    for n in (0, 1, 8, 9, 10, 11):
        bufs[n][...] = jnp.zeros_like(bufs[n])
    latin[:, :, 128:144, :] = jnp.zeros((2, 2, 16, D), BF16)

    class Scatter:
        def __init__(self, refs, w):
            (self.gw, self.r0, self.s1a, self.r1a, self.s1b, self.r1b,
             self.s2a, self.r2a, self.s2b, self.r2b, self.s3, self.r3) = refs
            self.left, self.right = slice(0, w), slice(w, 2 * w)
            self.cores = [
                remote(self.gw.at[:, flip(core), :, c], self.r0.at[:, :, c], twin)
                for c in (self.left, self.right)
            ]
            d3 = range(3)
            self.one_a = [remote(self.s1a.at[zs[d]], self.r1a.at[d], zdev[d]) for d in d3]
            self.one_b = [remote(self.s1b.at[ys[d]], self.r1b.at[d], ydev[d]) for d in d3]
            self.two_a = [remote(self.s2a.at[ys[d]], self.r2a.at[d], ydev[d]) for d in d3]
            self.two_b = [remote(self.s2b.at[zs[d]], self.r2b.at[d], zdev[d]) for d in d3]
            self.three = [remote(self.s3.at[xs[d]], self.r3.at[d], xdev[d]) for d in d3]

        def put(self, lo, grad):
            grad_scale = 1.0 / math.sqrt(CELLS * 128)
            self.gw[:, :, :, lo : lo + 256] = (grad * grad_scale).reshape(8, 2, 32, 256)

        def step1(self):
            self.cores[0].wait()
            for k in range(8):
                total = self.gw[k, core, :, self.left] + self.r0[k, :, self.left]
                self.gw[k, core, :, self.left] = total
                self.s1a[k // 2, k % 2] = total.astype(BF16)
            for copy in self.one_a:
                copy.start()
            self.cores[1].wait()
            for k in range(8):
                total = self.gw[k, core, :, self.right] + self.r0[k, :, self.right]
                self.gw[k, core, :, self.right] = total
                low = total.astype(BF16)
                for h in range(2):
                    self.s1b[k % 2, h, k // 2] = low[16 * h : 16 * h + 16]
            for copy in self.one_b:
                copy.start()

        def step2(self):
            for copy in self.one_a:
                copy.wait()
            for k in range(2):
                total = self.gw[z * 2 + k, core, :, self.left]
                for d in range(3):
                    total = total + self.r1a[d, k].astype(F32)
                for h in range(2):
                    self.s2a[k, h] = total[16 * h : 16 * h + 16]
            for copy in self.two_a:
                copy.start()
            for copy in self.one_b:
                copy.wait()
            mine = pl.ds(pl.multiple_of(yh * 16, 16), 16)
            for k in range(4):
                total = self.gw[k * 2 + yl, core, mine, self.right]
                for d in range(3):
                    total = total + self.r1b[d, k].astype(F32)
                self.s2b[k] = total
            for copy in self.two_b:
                copy.start()

        def step3(self):
            for copy in self.two_a + self.two_b:
                copy.wait()
            left, right = self.s2a[yl, yh], self.s2b[z]
            for d in range(3):
                left = left + self.r2a[d]
                right = right + self.r2b[d]
            for k in range(4):
                self.s3[k, 0:4, :] = left[4 * k : 4 * k + 4]
                self.s3[k, 4:8, :] = right[4 * k : 4 * k + 4]
            for copy in self.three:
                copy.start()

        def result(self):
            for copy in self.three:
                copy.wait()
            total = self.s3[x] + self.r3[0] + self.r3[1] + self.r3[2]
            return jnp.concatenate([total[0:4], total[4:8]], 1)

    early, final = Scatter(sums[0], 384), Scatter(sums[1], 640)

    def gather(a, strip, g, which):
        runs = groups(strip)[g]
        cells = [own[a, lev, c * 24 : (c + n) * 24, :] for lev, c, n in runs]
        lo, hi = which
        width = 192
        if hi == 4:
            cells += [halo[a, lev, c * 4 : (c + n) * 4, :] for lev, c, n in runs]
            width = 224
        got = dot(order[48 * lo : 48 * hi, :width], jnp.concatenate(cells, 0)).astype(BF16)
        for i in range(lo, hi):
            at = slot(strip, i) * WIN + g * 48
            (tw, cw)[a][at : at + 48, :] = got[(i - lo) * 48 : (i - lo) * 48 + 48]

    def project(first):
        @pl.loop(0, 3)
        def _(t):
            rows = pl.ds(first + t * 288, 288)
            cells = tw[rows, :].astype(F32)
            mu = jnp.mean(cells, -1, keepdims=True)
            cells = cells - mu
            iv = lax.rsqrt(jnp.mean(cells * cells, -1, keepdims=True) + EPS)
            h = (cells * iv * gain[...]).astype(BF16)
            hid[rows, :] = h
            mean[rows, :] = mu
            inv[rows, :] = iv
            for n in range(3):
                at = slice(512 * n, 512 * n + 512)
                proj[rows, at] = dot(h, wqkv[:, at]).astype(BF16)
            datt[rows, :] = dot(cw[rows, :], wo[...], NT).astype(BF16)

    res = (hid, datt)

    def outputs(first):
        @pl.loop(0, 3)
        def _(t):
            rows = pl.ds(first + t * 288, 288)
            cells = tw[rows, :].astype(F32)
            res[0][rows, :] = (cells + dot(att[rows, :], wo[...])).astype(BF16)
            u = dot(dproj[rows, :], wqkv[...], NT) * gain[...]
            iv = inv[rows, :]
            normed = (cells - mean[rows, :]) * iv
            d = u - jnp.mean(u, -1, keepdims=True)
            d = d - normed * jnp.mean(u * normed, -1, keepdims=True)
            res[1][rows, :] = (cw[rows, :].astype(F32) + iv * d).astype(BF16)

    def windows_of(a, strip, g):
        at = [slot(strip, i) * WIN + g * 48 for i in range(4)]
        return [res[a][n : n + 48, :] for n in at]

    for copy in loads:
        copy.wait()
    for a in range(2):
        for strip in range(2):
            for g in range(3):
                gather(a, strip, g, (0, 3))

    def pairs_of(a, level, column, count):
        got = []
        here = min(count, max(0, 30 - column))
        if here:
            got.append(own[a, level, column * 24 : (column + here) * 24, :])
        if count - here:
            c = column + here - 30
            got.append(edge[a, level, c * 24 : (c + count - here) * 24, :])
        return got

    for a in range(2):
        for level in range(2):
            for column, count in ((0, 8), (8, 8), (16, 8), (24, 8), (32, 4)):
                cells = jnp.concatenate(pairs_of(a, level, column, count), 0)
                small = dot(squeeze[: count * 4, : count * 24], cells).astype(BF16)
                lsend[a, level, column * 4 : (column + count) * 4, :] = small
    project(0)
    pl.semaphore_wait(barrier, 16)
    for copy in halo_in:
        copy.start()

    def receive_halo():
        for copy in halo_in:
            copy.wait()
        late_row = lax.broadcasted_iota(jnp.int32, (32, D), 0) >= 8
        for a in range(2):
            for level in range(2):
                halo[a, level, 112:144, :] = jnp.where(
                    late_row, corner[a, level], halo[a, level, 112:144, :]
                )
            for g in range(3):
                for strip in range(2):
                    gather(a, strip, g, (3, 4))
                gather(a, 2, g, (0, 4))
        project(864)

    def return_halo():
        hidt[...] = hid[...].T
        outputs(864)
        for a in range(2):
            for strip in range(3):
                for g, runs in enumerate(groups(strip)):
                    if strip == 2:
                        cells = windows_of(a, strip, g)
                        whole = dot(place[:, :192], jnp.concatenate(cells, 0)).astype(BF16)
                    at = slot(strip, 3) * WIN + g * 48
                    small = dot(late[...], res[a][at : at + 48, :]).astype(BF16)
                    at = 0
                    for lev, c, n in runs:
                        lout[a, lev, c * 4 : (c + n) * 4, :] = small[at * 4 : (at + n) * 4]
                        if strip == 2:
                            to = slice((c - 24) * 24, (c - 24 + n) * 24)
                            region[a, lev, to, :] = whole[at * 24 : (at + n) * 24]
                        at += n
            for copy in halo_out[3 * a : 3 * a + 3]:
                copy.start()
        for n in range(3):
            early.put(256 * n, dot(hidt[...], dproj[:, 512 * n : 512 * n + 256]))
            if n:
                early.cores[n - 1].start()

    @pl.loop(0, 4)
    def _(part):
        pl.when(part == 1)(receive_halo)
        pl.when(part == 3)(return_halo)
        lo = jnp.where(part >= 2, 256, 0)
        first = jnp.where(jnp.logical_or(part == 1, part == 2), 6, 0)
        key_side = (lax.broadcasted_iota(jnp.int32, (WIN, 1), 0) % 6) >= 3
        lane = lax.broadcasted_iota(jnp.int32, (1, 256), 1)
        query = jnp.where(lane < 128, lane, 128 + lane % 16)
        differ = key_side != ((query % 6) >= 3)

        @pl.loop(0, 6)
        def _(i):
            w = first + i
            last = jnp.logical_or(jnp.logical_or(w == 6, w == 7), w == 11)
            apart = jnp.logical_and(last, lat == lats - 1)
            bias[...] = jnp.where(jnp.logical_and(apart, differ), -1e30, 0.0)
            attend(w, lo, proj, datt, bias, hm, hmf, att, dproj, bufs)
            pl.when(jnp.logical_and(part == 3, i == 1))(early.step1)

    attt[...] = att[...].T
    for n in range(5):
        if n < 3:
            grad = dot(hidt[...], dproj[:, 512 * n + 256 : 512 * n + 512])
        else:
            grad = dot(attt[...], cw[:, 256 * n - 768 : 256 * n - 512])
        final.put(256 * n, grad)
        if n in (2, 4):
            final.cores[n // 2 - 1].start()
    early.step2()
    outputs(0)
    final.step1()
    early.step3()

    for copy in halo_out:
        copy.wait()
    for a in range(2):
        for level in range(2):
            edge_in = jnp.concatenate([lonin[a, level], cornerin[a, level]], 0)
            edge[a, level] = dot(fill[...], edge_in).astype(BF16)
        for strip in range(3):
            for g, runs in enumerate(groups(strip)):
                cells = windows_of(a, strip, g)
                cells += [latin[a, lev, c * 4 : (c + n) * 4, :] for lev, c, n in runs]
                whole = dot(place[...], jnp.concatenate(cells, 0)).astype(BF16)
                at = 0
                for lev, c, n in runs:
                    keep = min(n, max(0, 30 - c))
                    if keep:
                        own[a, lev, c * 24 : (c + keep) * 24, :] = whole[at * 24 : (at + keep) * 24]
                    at += n
    stores = []
    for a, ref in enumerate((out, dtok)):
        stores.append(
            pltpu.make_async_copy(own.at[a, :, 0:720], ref.at[:, 144:864], local.at[2 * a])
        )
        stores.append(pltpu.make_async_copy(edge.at[a], ref.at[:, 0:144], local.at[2 * a + 1]))
    for copy in stores:
        copy.start()

    grads = early.result()
    for n in range(3):
        dqkv[:, 512 * n : 512 * n + 256] = grads[:, 256 * n : 256 * n + 256]
    final.step2()
    final.step3()
    grads = final.result()
    for n in range(3):
        dqkv[:, 512 * n + 256 : 512 * n + 512] = grads[:, 256 * n : 256 * n + 256]
    dwo[...] = grads[:, 768:1280]
    for copy in stores:
        copy.wait()


def per_device(tokens, gain, qkv_weight, out_weight, cotangent):
    by_column = lambda a: a.transpose(0, 2, 1, 3).reshape(2, 864, D)
    vmem = pl.BlockSpec(memory_space=pltpu.VMEM)
    hbm = pl.BlockSpec(memory_space=pl.ANY)
    shape = jax.ShapeDtypeStruct
    buf = lambda *dims: pltpu.VMEM(dims, BF16)
    buf32 = lambda *dims: pltpu.VMEM(dims, F32)
    consts = tables()
    copies = 12 + 2 * (2 + 6 + 6 + 3)

    def scatter(w):
        return [
            buf32(8, 2, 32, 2 * w),
            buf32(8, 32, 2 * w),
            buf(4, 2, 32, w),
            buf(3, 2, 32, w),
            buf(2, 2, 4, 16, w),
            buf(3, 4, 16, w),
            buf32(2, 2, 16, w),
            buf32(3, 16, w),
            buf32(4, 16, w),
            buf32(3, 16, w),
            buf32(4, 8, w),
            buf32(3, 8, w),
        ]

    out, dtok, dqkv, dwo = pl.pallas_call(
        kernel,
        out_shape=(
            shape((2, 864, D), BF16),
            shape((2, 864, D), BF16),
            shape((4, 3 * D), F32),
            shape((4, D), F32),
        ),
        in_specs=[hbm, hbm] + [vmem] * (3 + len(consts)),
        out_specs=(hbm, hbm, vmem, vmem),
        scratch_shapes=[
            buf(2, 2, 864, D),
            buf(2, 2, 144, D),
            buf(2, 2, 144, D),
            buf(2, 2, 32, D),
            buf(2, 2, 144, D),
            buf(2, 2, 288, D),
            buf(2, 2, 144, D),
            buf(2, 2, 144, D),
            buf(2, 2, 144, D),
            buf(2, 2, 32, D),
            buf(CELLS, D),
            buf(CELLS, D),
            buf(CELLS, D),
            buf(D, CELLS),
            buf(D, CELLS),
            buf32(CELLS, 1),
            buf32(CELLS, 1),
            buf(CELLS, 3 * D),
            buf(CELLS, D),
            buf(CELLS, D),
            buf(CELLS, 3 * D),
            buf32(WIN, 256),
            *[buf(256, 1152)] * 2,
            *[buf32(WIN, 1152)] * 2,
            *[buf(WIN, 1152)] * 2,
            *[buf(128, 1152)] * 2,
            *[buf(1152, 256)] * 4,
            *scatter(384),
            *scatter(640),
            pltpu.SemaphoreType.DMA((4,)),
            pltpu.SemaphoreType.DMA((copies,)),
            pltpu.SemaphoreType.DMA((copies,)),
        ],
        compiler_params=pltpu.CompilerParams(
            collective_id=0, has_side_effects=True, vmem_limit_bytes=60 * 2**20
        ),
        name="block",
    )(
        by_column(tokens),
        by_column(cotangent),
        gain.reshape(1, D),
        qkv_weight,
        out_weight,
        *consts,
    )
    in_place = lambda a: a.reshape(2, 36, 24, D).transpose(0, 2, 1, 3)
    return in_place(out), in_place(dtok), dqkv, dwo


def solution(mesh):
    in_specs = (P(None, "lat", "lon", None), P(), P(), P(), P(None, "lat", "lon", None))
    out_specs = (
        P(None, "lat", "lon", None),
        P(None, "lat", "lon", None),
        P(("lon", "lat"), None),
        P(("lon", "lat"), None),
    )
    return jax.shard_map(
        per_device, mesh=mesh, in_specs=in_specs, out_specs=out_specs, check_vma=False
    )
```

time: 113 us -> 98.7 us (0.87)
  Pallas kernels: 107 us -> 92 us
    pallas_call x1, Pallas kernels: 107 us -> 92 us  [per_device(): pl.pallas_call(kernel, out_shape=(shape((2, 864, D), BF16), shape((2, 864...]
where the time goes in v2:
time: 98.7 us; the launch traced here: 98.1 us
  Pallas kernels  92 us (93%)
  local copies, waits for them, and re-layouts  5.36 us (5%)
    pallas_call x1, Pallas kernels, per_device(): pl.pallas_call(kernel, out_shape=(shape((2, 864, D), BF16), shape((2, 864...  92 us
    unnamed x10, local copies, waits for them, and re-layouts  5.36 us

profile of v2, /device:TPU:1, one launch (start us, length us, event | category | flops | bytes accessed | tf_op | source)
XLA Modules:
  0.0 98.1 jit_solution(17357934497422067394)
XLA Ops:
  0.6 92.0 %block.1 = (bf16[2,864,512]{2,1,0:T(8,128)(2,1)}, bf16[2,864,512]{2,1,0:T(8,128)(2,1)}, f32[4,1536]{1,0:T(4,128)}, f32[4,512]{1,0:T(4,128)}) custom-call(bf16[2,864,512]{2,1,0:T(8,128)(2,1)} %bitcast.13, bf16[2,864,512]{2,1,0:T(8,128)(2,1)} %bitcast.14, f32[1,512]{1,0:T(1,128)} %bitcast.17, bf16[512,1536]{1,0:T(8,128)(2,1)} %wqkv.1, bf16[512,512]{1,0:T(8,128)(2,1)} %wo.1, ...), custom_call_target="tpu_custom_call" | custom-call | tf_op jit(solution)/shard_map/block/pallas_call | solution.py:495
  92.7 0.0 copy-start
  92.7 2.9 %copy.20 = bf16[2,24,36,512]{3,1,2,0:T(8,128)(2,1)} copy(bf16[2,24,36,512]{3,1,2,0:T(8,128)(2,1)} %bitcast.16) | data formatting | bytes 3538944
  95.6 0.0 copy-done
  95.6 0.0 copy-start.1
  95.6 0.0 copy-start.2
  95.6 1.2 %copy.21 = bf16[2,24,36,512]{3,1,2,0:T(8,128)(2,1)} copy(bf16[2,24,36,512]{3,1,2,0:T(8,128)(2,1)S(1)} %bitcast.15) | data formatting | bytes 3538944
  96.8 0.0 copy-done.1
  96.9 0.6 copy.22
  97.5 0.0 copy-done.2
  97.5 0.6 copy.23
Async XLA Ops:
  92.7 2.9 %copy-start = (bf16[2,864,512]{2,1,0:T(8,128)(2,1)S(1)}, bf16[2,864,512]{2,1,0:T(8,128)(2,1)}, u32[]{:S(2)}) copy-start(bf16[2,864,512]{2,1,0:T(8,128)(2,1)} %get-tuple-element.9) | copy-start | bytes 5308420
  95.6 1.2 %copy-start.1 = (f32[4,1536]{1,0:T(4,128)S(1)}, f32[4,1536]{1,0:T(4,128)}, u32[]{:S(2)}) copy-start(f32[4,1536]{1,0:T(4,128)} %get-tuple-element.18) | copy-start | bytes 73732
  95.6 1.8 %copy-start.2 = (f32[4,512]{1,0:T(4,128)S(1)}, f32[4,512]{1,0:T(4,128)}, u32[]{:S(2)}) copy-start(f32[4,512]{1,0:T(4,128)} %get-tuple-element.19) | copy-start | bytes 24580

commit v3 on v2

--- a/solution.py
+++ b/solution.py
@@ -27,42 +27,43 @@
     return lax.dot_general(a, b, dims, preferred_element_type=F32)
 
 
+def groups(strip):
+    c = 12 * strip
+    return [[(0, c, 8)], [(0, c + 8, 4), (1, c, 4)], [(1, c + 4, 8)]]
+
+
 def tables():
-    order = np.zeros((192, 224), np.float32)
-    place = np.zeros((192, 224), np.float32)
-    squeeze = np.zeros((32, 192), np.float32)
-    late = np.zeros((32, 48), np.float32)
-    fill = np.zeros((144, 176), np.float32)
+    order = np.zeros((192, 192), np.float32)
+    squeeze = np.zeros((48, 384), np.float32)
+    last = np.zeros((432, 240), np.float32)
+    spread = np.zeros((480, 192), np.float32)
     for c in range(8):
-        for rho in range(24):
-            cell = (rho // 6) * 48 + c * 6 + rho % 6
-            if rho < 21:
-                order[cell, c * 24 + 3 + rho] = 1
-                place[c * 24 + 3 + rho, cell] = 1
-            else:
-                order[cell, 192 + c * 4 + rho - 21] = 1
-                place[c * 24 + rho - 21, 192 + c * 4 + rho - 21] = 1
-                late[c * 4 + rho - 21, c * 6 + rho % 6] = 1
-                squeeze[c * 4 + rho - 21, c * 24 + rho - 21] = 1
-    for c in range(6):
-        for row in range(24):
-            fill[c * 24 + row, c * 24 + row if row >= 3 else 144 + 8 + c * 4 + row] = 1
+        for rho in range(21):
+            order[(rho // 6) * 48 + c * 6 + rho % 6, c * 24 + 3 + rho] = 1
+    for c in range(16):
+        for r in range(3):
+            squeeze[c * 3 + r, c * 24 + r] = 1
+    for c in range(60):
+        for r in range(3):
+            spread[c * 8 + r, c * 3 + r] = 1
+    for strip in range(3):
+        for g, runs in enumerate(groups(strip)):
+            pairs = [(lev, c + i) for lev, c, n in runs for i in range(n)]
+            for p, (lev, c) in enumerate(pairs):
+                at = (lev * 30 + c) * 3 if c < 30 else 192 + (lev * 6 + c - 30) * 3
+                for r in range(3):
+                    last[strip * 144 + g * 48 + p * 6 + 3 + r, at + r] = 1
     heads = np.zeros((128, 256), np.float32)
     for h in range(8):
         heads[16 * h : 16 * h + 16, 32 * h : 32 * h + 32] = 1
-    bf = [jnp.asarray(t, BF16) for t in (order, place, squeeze, late, fill, heads)]
+    bf = [jnp.asarray(t, BF16) for t in (order, order.T, squeeze, last, last.T, spread, heads)]
     return bf + [jnp.asarray(heads, F32)]
 
 
-def groups(strip):
-    c = 12 * strip
-    return [[(0, c, 8)], [(0, c + 8, 4), (1, c, 4)], [(1, c + 4, 8)]]
-
-
 def slot(strip, i):
-    if strip < 2:
-        return strip * 3 + i if i < 3 else 6 + strip
-    return 8 + i
+    if i == 3:
+        return 9 + strip
+    return strip * 3 + i
 
 
 def masked_tail(x, hm):
@@ -130,14 +131,14 @@
 
 
 def kernel(
-    tok, cot, gain, wqkv, wo, order, place, squeeze, late, fill, hm, hmf,
+    tok, cot, gain, wqkv, wo, order, place, squeeze, late, late_t, spread, hm, hmf,
     out, dtok, dqkv, dwo,
-    own, edge, halo, corner, lsend, region, lout, lonin, latin, cornerin,
+    own, edge, halo, lsend, region, lout, lonin, latin,
     tw, cw, hid, hidt, attt, inv, mean, proj, datt, att, dproj, bias, *more,
 ):
     bufs, more = more[:12], more[12:]
-    sums = (more[:12], more[12:24])
-    local, send, recv = more[24:]
+    sums = (more[:13], more[13:26])
+    local, send, recv = more[26:]
     lon, lat = lax.axis_index("lon"), lax.axis_index("lat")
     lons, lats = lax.axis_size("lon"), lax.axis_size("lat")
     z, yl, core = lon // 4, (lon // 2) % 2, lon % 2
@@ -185,23 +186,22 @@
     halo_in, halo_out = [], []
     for a, ref in enumerate((tok, cot)):
         halo_in.append(remote(ref.at[:, 0:144], own.at[a, :, 720:864], dev(west, lat)))
-        halo_in.append(remote(lsend.at[a, :, 0:128], halo.at[a, :, 0:128], dev(lon, south)))
-        halo_in.append(remote(lsend.at[a, :, 112:144], corner.at[a], dev(west, south)))
         halo_out.append(remote(region.at[a, :, 144:288], lonin.at[a], dev(east, lat)))
-        halo_out.append(remote(lout.at[a, :, 0:128], latin.at[a, :, 0:128], dev(lon, north)))
-        halo_out.append(remote(lout.at[a, :, 112:144], cornerin.at[a], dev(east, north)))
+    for a in range(2):
+        for rows, lon_in, lon_out in ((slice(0, 192), lon, lon), (slice(192, 240), west, east)):
+            halo_in.append(remote(lsend.at[a, rows], halo.at[a, rows], dev(lon_in, south)))
+            halo_out.append(remote(lout.at[a, rows], latin.at[a, rows], dev(lon_out, north)))
 
     for n in (0, 1, 8, 9, 10, 11):
         bufs[n][...] = jnp.zeros_like(bufs[n])
-    latin[:, :, 128:144, :] = jnp.zeros((2, 2, 16, D), BF16)
 
     class Scatter:
         def __init__(self, refs, w):
-            (self.gw, self.r0, self.s1a, self.r1a, self.s1b, self.r1b,
+            (self.gw, self.s0, self.r0, self.s1a, self.r1a, self.s1b, self.r1b,
              self.s2a, self.r2a, self.s2b, self.r2b, self.s3, self.r3) = refs
             self.left, self.right = slice(0, w), slice(w, 2 * w)
             self.cores = [
-                remote(self.gw.at[:, flip(core), :, c], self.r0.at[:, :, c], twin)
+                remote(self.s0.at[:, :, c], self.r0.at[:, :, c], twin)
                 for c in (self.left, self.right)
             ]
             d3 = range(3)
@@ -213,20 +213,23 @@
 
         def put(self, lo, grad):
             grad_scale = 1.0 / math.sqrt(CELLS * 128)
-            self.gw[:, :, :, lo : lo + 256] = (grad * grad_scale).reshape(8, 2, 32, 256)
+            grad = (grad * grad_scale).reshape(8, 2, 32, 256)
+            one, two = grad[:, 0], grad[:, 1]
+            self.gw[:, :, lo : lo + 256] = jnp.where(core == 0, one, two)
+            self.s0[:, :, lo : lo + 256] = jnp.where(core == 0, two, one).astype(BF16)
 
         def step1(self):
             self.cores[0].wait()
             for k in range(8):
-                total = self.gw[k, core, :, self.left] + self.r0[k, :, self.left]
-                self.gw[k, core, :, self.left] = total
+                total = self.gw[k, :, self.left] + self.r0[k, :, self.left].astype(F32)
+                self.gw[k, :, self.left] = total
                 self.s1a[k // 2, k % 2] = total.astype(BF16)
             for copy in self.one_a:
                 copy.start()
             self.cores[1].wait()
             for k in range(8):
-                total = self.gw[k, core, :, self.right] + self.r0[k, :, self.right]
-                self.gw[k, core, :, self.right] = total
+                total = self.gw[k, :, self.right] + self.r0[k, :, self.right].astype(F32)
+                self.gw[k, :, self.right] = total
                 low = total.astype(BF16)
                 for h in range(2):
                     self.s1b[k % 2, h, k // 2] = low[16 * h : 16 * h + 16]
@@ -237,7 +240,7 @@
             for copy in self.one_a:
                 copy.wait()
             for k in range(2):
-                total = self.gw[z * 2 + k, core, :, self.left]
+                total = self.gw[z * 2 + k, :, self.left]
                 for d in range(3):
                     total = total + self.r1a[d, k].astype(F32)
                 for h in range(2):
@@ -248,7 +251,7 @@
                 copy.wait()
             mine = pl.ds(pl.multiple_of(yh * 16, 16), 16)
             for k in range(4):
-                total = self.gw[k * 2 + yl, core, mine, self.right]
+                total = self.gw[k * 2 + yl, mine, self.right]
                 for d in range(3):
                     total = total + self.r1b[d, k].astype(F32)
                 self.s2b[k] = total
@@ -276,23 +279,22 @@
 
     early, final = Scatter(sums[0], 384), Scatter(sums[1], 640)
 
-    def gather(a, strip, g, which):
+    def rows_of(a, strip, g):
         runs = groups(strip)[g]
-        cells = [own[a, lev, c * 24 : (c + n) * 24, :] for lev, c, n in runs]
-        lo, hi = which
-        width = 192
-        if hi == 4:
-            cells += [halo[a, lev, c * 4 : (c + n) * 4, :] for lev, c, n in runs]
-            width = 224
-        got = dot(order[48 * lo : 48 * hi, :width], jnp.concatenate(cells, 0)).astype(BF16)
-        for i in range(lo, hi):
-            at = slot(strip, i) * WIN + g * 48
-            (tw, cw)[a][at : at + 48, :] = got[(i - lo) * 48 : (i - lo) * 48 + 48]
-
-    def project(first):
-        @pl.loop(0, 3)
+        return jnp.concatenate([own[a, v, c * 24 : (c + n) * 24, :] for v, c, n in runs], 0)
+
+    def gather(strip):
+        for a in range(2):
+            for g in range(3):
+                got = dot(order[:144, :], rows_of(a, strip, g)).astype(BF16)
+                for i in range(3):
+                    at = slot(strip, i) * WIN + g * 48
+                    (tw, cw)[a][at : at + 48, :] = got[i * 48 : i * 48 + 48]
+
+    def project(first, chunks):
+        @pl.loop(0, chunks)
         def _(t):
-            rows = pl.ds(first + t * 288, 288)
+            rows = pl.ds(pl.multiple_of(first + t * 432, 16), 432)
             cells = tw[rows, :].astype(F32)
             mu = jnp.mean(cells, -1, keepdims=True)
             cells = cells - mu
@@ -309,9 +311,9 @@
     res = (hid, datt)
 
     def outputs(first):
-        @pl.loop(0, 3)
+        @pl.loop(0, 2)
         def _(t):
-            rows = pl.ds(first + t * 288, 288)
+            rows = pl.ds(pl.multiple_of(first + t * 432, 16), 432)
             cells = tw[rows, :].astype(F32)
             res[0][rows, :] = (cells + dot(att[rows, :], wo[...])).astype(BF16)
             u = dot(dproj[rows, :], wqkv[...], NT) * gain[...]
@@ -327,92 +329,82 @@
 
     for copy in loads:
         copy.wait()
+    gather(0)
+    gather(1)
     for a in range(2):
-        for strip in range(2):
-            for g in range(3):
-                gather(a, strip, g, (0, 3))
-
-    def pairs_of(a, level, column, count):
-        got = []
-        here = min(count, max(0, 30 - column))
-        if here:
-            got.append(own[a, level, column * 24 : (column + here) * 24, :])
-        if count - here:
-            c = column + here - 30
-            got.append(edge[a, level, c * 24 : (c + count - here) * 24, :])
-        return got
-
-    for a in range(2):
-        for level in range(2):
-            for column, count in ((0, 8), (8, 8), (16, 8), (24, 8), (32, 4)):
-                cells = jnp.concatenate(pairs_of(a, level, column, count), 0)
-                small = dot(squeeze[: count * 4, : count * 24], cells).astype(BF16)
-                lsend[a, level, column * 4 : (column + count) * 4, :] = small
-    project(0)
+        lead = [own[a, 0, 0:384, :]]
+        lead += [jnp.concatenate([own[a, 0, 384:720, :], own[a, 1, 0:48, :]], 0)]
+        lead += [own[a, 1, 48:432, :], own[a, 1, 432:720, :]]
+        lead += [jnp.concatenate([edge[a, 0], edge[a, 1]], 0)]
+        for n, cells in enumerate(lead):
+            small = dot(squeeze[:, : cells.shape[0]], cells).astype(BF16)
+            lsend[a, 48 * n : 48 * n + 48, :] = small
+    project(0, 2)
     pl.semaphore_wait(barrier, 16)
     for copy in halo_in:
         copy.start()
 
-    def receive_halo():
-        for copy in halo_in:
+    def receive_columns():
+        for copy in halo_in[:2]:
             copy.wait()
-        late_row = lax.broadcasted_iota(jnp.int32, (32, D), 0) >= 8
+        gather(2)
+        project(864, 1)
+
+    def receive_rows():
+        for copy in halo_in[2:]:
+            copy.wait()
         for a in range(2):
-            for level in range(2):
-                halo[a, level, 112:144, :] = jnp.where(
-                    late_row, corner[a, level], halo[a, level, 112:144, :]
-                )
-            for g in range(3):
-                for strip in range(2):
-                    gather(a, strip, g, (3, 4))
-                gather(a, 2, g, (0, 4))
-        project(864)
-
-    def return_halo():
+            base = dot(late[...], halo[a])
+            for strip in range(3):
+                for g in range(3):
+                    at = strip * WIN + g * 48
+                    got = dot(order[144:192, :], rows_of(a, strip, g)) + base[at : at + 48]
+                    (tw, cw)[a][1296 + at : 1344 + at, :] = got.astype(BF16)
+        project(1296, 1)
+
+    def first_gradients():
         hidt[...] = hid[...].T
-        outputs(864)
-        for a in range(2):
-            for strip in range(3):
-                for g, runs in enumerate(groups(strip)):
-                    if strip == 2:
-                        cells = windows_of(a, strip, g)
-                        whole = dot(place[:, :192], jnp.concatenate(cells, 0)).astype(BF16)
-                    at = slot(strip, 3) * WIN + g * 48
-                    small = dot(late[...], res[a][at : at + 48, :]).astype(BF16)
-                    at = 0
-                    for lev, c, n in runs:
-                        lout[a, lev, c * 4 : (c + n) * 4, :] = small[at * 4 : (at + n) * 4]
-                        if strip == 2:
-                            to = slice((c - 24) * 24, (c - 24 + n) * 24)
-                            region[a, lev, to, :] = whole[at * 24 : (at + n) * 24]
-                        at += n
-            for copy in halo_out[3 * a : 3 * a + 3]:
-                copy.start()
         for n in range(3):
             early.put(256 * n, dot(hidt[...], dproj[:, 512 * n : 512 * n + 256]))
             if n:
                 early.cores[n - 1].start()
 
-    @pl.loop(0, 4)
+    def return_halo():
+        for a in range(2):
+            lout[a] = dot(late_t[...], res[a][1296:1728, :]).astype(BF16)
+            for g, runs in enumerate(groups(2)):
+                cells = windows_of(a, 2, g)
+                whole = dot(place[...], jnp.concatenate(cells, 0)).astype(BF16)
+                at = 0
+                for lev, c, n in runs:
+                    to = slice((c - 24) * 24, (c - 24 + n) * 24)
+                    region[a, lev, to, :] = whole[at * 24 : (at + n) * 24]
+                    at += n
+        for copy in halo_out:
+            copy.start()
+
+    @pl.loop(0, 6)
     def _(part):
-        pl.when(part == 1)(receive_halo)
-        pl.when(part == 3)(return_halo)
-        lo = jnp.where(part >= 2, 256, 0)
-        first = jnp.where(jnp.logical_or(part == 1, part == 2), 6, 0)
+        pl.when(part == 2)(receive_columns)
+        pl.when(part == 4)(receive_rows)
+        pl.when(part == 5)(first_gradients)
+        lo = (part % 2) * 256
+        first = jnp.where(part < 2, 0, jnp.where(part < 4, 6, 9))
+        count = jnp.where(part < 2, 6, 3)
         key_side = (lax.broadcasted_iota(jnp.int32, (WIN, 1), 0) % 6) >= 3
         lane = lax.broadcasted_iota(jnp.int32, (1, 256), 1)
         query = jnp.where(lane < 128, lane, 128 + lane % 16)
         differ = key_side != ((query % 6) >= 3)
-
-        @pl.loop(0, 6)
-        def _(i):
-            w = first + i
-            last = jnp.logical_or(jnp.logical_or(w == 6, w == 7), w == 11)
-            apart = jnp.logical_and(last, lat == lats - 1)
-            bias[...] = jnp.where(jnp.logical_and(apart, differ), -1e30, 0.0)
+        apart = jnp.logical_and(part >= 4, lat == lats - 1)
+        bias[...] = jnp.where(jnp.logical_and(apart, differ), -1e30, 0.0)
+
+        @pl.loop(first, first + count)
+        def _(w):
             attend(w, lo, proj, datt, bias, hm, hmf, att, dproj, bufs)
-            pl.when(jnp.logical_and(part == 3, i == 1))(early.step1)
-
+
+    early.step1()
+    outputs(864)
+    return_halo()
     attt[...] = att[...].T
     for n in range(5):
         if n < 3:
@@ -426,23 +418,38 @@
     outputs(0)
     final.step1()
     early.step3()
+    final.step2()
+    grads = early.result()
+    for n in range(3):
+        dqkv[:, 512 * n : 512 * n + 256] = grads[:, 256 * n : 256 * n + 256]
+    final.step3()
 
     for copy in halo_out:
         copy.wait()
+
+    def with_first(cells, first):
+        cells = cells.reshape(-1, 24, D)
+        first = first.reshape(-1, 8, D)
+        cells = jnp.concatenate([cells[:, 0:8] + first, cells[:, 8:24]], 1)
+        return cells.reshape(-1, D).astype(BF16)
+
     for a in range(2):
+        rows = dot(spread[:96, :48], latin[a, 192:240, :])
         for level in range(2):
-            edge_in = jnp.concatenate([lonin[a, level], cornerin[a, level]], 0)
-            edge[a, level] = dot(fill[...], edge_in).astype(BF16)
+            cells = lonin[a, level].astype(F32)
+            edge[a, level] = with_first(cells, rows[48 * level : 48 * level + 48])
+        rows = dot(spread[...], latin[a, 0:192, :])
         for strip in range(3):
             for g, runs in enumerate(groups(strip)):
                 cells = windows_of(a, strip, g)
-                cells += [latin[a, lev, c * 4 : (c + n) * 4, :] for lev, c, n in runs]
-                whole = dot(place[...], jnp.concatenate(cells, 0)).astype(BF16)
+                whole = dot(place[...], jnp.concatenate(cells, 0))
                 at = 0
                 for lev, c, n in runs:
                     keep = min(n, max(0, 30 - c))
                     if keep:
-                        own[a, lev, c * 24 : (c + keep) * 24, :] = whole[at * 24 : (at + keep) * 24]
+                        top = (lev * 30 + c) * 8
+                        part = with_first(whole[at * 24 : (at + keep) * 24], rows[top : top + 8 * keep])
+                        own[a, lev, c * 24 : (c + keep) * 24, :] = part
                     at += n
     stores = []
     for a, ref in enumerate((out, dtok)):
@@ -453,11 +460,6 @@
     for copy in stores:
         copy.start()
 
-    grads = early.result()
-    for n in range(3):
-        dqkv[:, 512 * n : 512 * n + 256] = grads[:, 256 * n : 256 * n + 256]
-    final.step2()
-    final.step3()
     grads = final.result()
     for n in range(3):
         dqkv[:, 512 * n + 256 : 512 * n + 512] = grads[:, 256 * n : 256 * n + 256]
@@ -478,8 +480,9 @@
 
     def scatter(w):
         return [
-            buf32(8, 2, 32, 2 * w),
             buf32(8, 32, 2 * w),
+            buf(8, 32, 2 * w),
+            buf(8, 32, 2 * w),
             buf(4, 2, 32, w),
             buf(3, 2, 32, w),
             buf(2, 2, 4, 16, w),
@@ -505,14 +508,12 @@
         scratch_shapes=[
             buf(2, 2, 864, D),
             buf(2, 2, 144, D),
+            buf(2, 240, D),
+            buf(2, 240, D),
+            buf(2, 2, 288, D),
+            buf(2, 240, D),
             buf(2, 2, 144, D),
-            buf(2, 2, 32, D),
-            buf(2, 2, 144, D),
-            buf(2, 2, 288, D),
-            buf(2, 2, 144, D),
-            buf(2, 2, 144, D),
-            buf(2, 2, 144, D),
-            buf(2, 2, 32, D),
+            buf(2, 240, D),
             buf(CELLS, D),
             buf(CELLS, D),
             buf(CELLS, D),

time: 98.7 us -> 91.2 us (0.924)
  Pallas kernels: 92 us -> 85.1 us
    pallas_call x1, Pallas kernels: 92 us -> 85.1 us  [per_device(): pl.pallas_call(kernel, out_shape=(shape((2, 864, D), BF16), shape((2, 864...]
where the time goes in v3:
time: 91.2 us; the launch traced here: 91.1 us
  Pallas kernels  85.1 us (93%)
  local copies, waits for them, and re-layouts  5.36 us (6%)
    pallas_call x1, Pallas kernels, per_device(): pl.pallas_call(kernel, out_shape=(shape((2, 864, D), BF16), shape((2, 864...  85.1 us
    unnamed x10, local copies, waits for them, and re-layouts  5.36 us

profile of v3, /device:TPU:1, one launch (start us, length us, event | category | flops | bytes accessed | tf_op | source)
XLA Modules:
  0.0 91.1 jit_solution(16990587620672926286)
XLA Ops:
  0.6 85.1 %block.1 = (bf16[2,864,512]{2,1,0:T(8,128)(2,1)}, bf16[2,864,512]{2,1,0:T(8,128)(2,1)}, f32[4,1536]{1,0:T(4,128)}, f32[4,512]{1,0:T(4,128)}) custom-call(bf16[2,864,512]{2,1,0:T(8,128)(2,1)} %bitcast.13, bf16[2,864,512]{2,1,0:T(8,128)(2,1)} %bitcast.14, f32[1,512]{1,0:T(1,128)} %bitcast.17, bf16[512,1536]{1,0:T(8,128)(2,1)} %wqkv.1, bf16[512,512]{1,0:T(8,128)(2,1)} %wo.1, ...), custom_call_target="tpu_custom_call" | custom-call | tf_op jit(solution)/shard_map/block/pallas_call | solution.py:498
  85.7 0.0 copy-start
  85.7 2.9 %copy.21 = bf16[2,24,36,512]{3,1,2,0:T(8,128)(2,1)} copy(bf16[2,24,36,512]{3,1,2,0:T(8,128)(2,1)} %bitcast.16) | data formatting | bytes 3538944
  88.6 0.0 copy-done
  88.6 0.0 copy-start.1
  88.6 0.0 copy-start.2
  88.6 1.2 %copy.22 = bf16[2,24,36,512]{3,1,2,0:T(8,128)(2,1)} copy(bf16[2,24,36,512]{3,1,2,0:T(8,128)(2,1)S(1)} %bitcast.15) | data formatting | bytes 3538944
  89.8 0.0 copy-done.1
  89.9 0.6 copy.23
  90.5 0.0 copy-done.2
  90.5 0.6 copy.24
Async XLA Ops:
  85.7 2.9 %copy-start = (bf16[2,864,512]{2,1,0:T(8,128)(2,1)S(1)}, bf16[2,864,512]{2,1,0:T(8,128)(2,1)}, u32[]{:S(2)}) copy-start(bf16[2,864,512]{2,1,0:T(8,128)(2,1)} %get-tuple-element.9) | copy-start | bytes 5308420
  88.6 1.2 %copy-start.1 = (f32[4,1536]{1,0:T(4,128)S(1)}, f32[4,1536]{1,0:T(4,128)}, u32[]{:S(2)}) copy-start(f32[4,1536]{1,0:T(4,128)} %get-tuple-element.18) | copy-start | bytes 73732
  88.6 1.8 %copy-start.2 = (f32[4,512]{1,0:T(4,128)S(1)}, f32[4,512]{1,0:T(4,128)}, u32[]{:S(2)}) copy-start(f32[4,512]{1,0:T(4,128)} %get-tuple-element.19) | copy-start | bytes 24580

commit v4 on v3

--- a/solution.py
+++ b/solution.py
@@ -131,14 +131,14 @@
 
 
 def kernel(
-    tok, cot, gain, wqkv, wo, order, place, squeeze, late, late_t, spread, hm, hmf,
-    out, dtok, dqkv, dwo,
-    own, edge, halo, lsend, region, lout, lonin, latin,
+    tok, cot, gain, wqkv, wo, order, place, squeeze, late, late_t, hm, hmf,
+    by_window, lonin, latin, dqkv, dwo,
+    own, edge, halo, lsend, region, lout,
     tw, cw, hid, hidt, attt, inv, mean, proj, datt, att, dproj, bias, *more,
 ):
     bufs, more = more[:12], more[12:]
-    sums = (more[:13], more[13:26])
-    local, send, recv = more[26:]
+    sums = (more[:14], more[14:28])
+    local, send, recv = more[28:]
     lon, lat = lax.axis_index("lon"), lax.axis_index("lat")
     lons, lats = lax.axis_size("lon"), lax.axis_size("lat")
     z, yl, core = lon // 4, (lon // 2) % 2, lon % 2
@@ -198,7 +198,7 @@
     class Scatter:
         def __init__(self, refs, w):
             (self.gw, self.s0, self.r0, self.s1a, self.r1a, self.s1b, self.r1b,
-             self.s2a, self.r2a, self.s2b, self.r2b, self.s3, self.r3) = refs
+             self.s2a, self.r2a, self.s2b, self.r2b, self.s3, self.r3, self.own_b) = refs
             self.left, self.right = slice(0, w), slice(w, 2 * w)
             self.cores = [
                 remote(self.s0.at[:, :, c], self.r0.at[:, :, c], twin)
@@ -206,10 +206,10 @@
             ]
             d3 = range(3)
             self.one_a = [remote(self.s1a.at[zs[d]], self.r1a.at[d], zdev[d]) for d in d3]
-            self.one_b = [remote(self.s1b.at[ys[d]], self.r1b.at[d], ydev[d]) for d in d3]
-            self.two_a = [remote(self.s2a.at[ys[d]], self.r2a.at[d], ydev[d]) for d in d3]
+            self.one_b = [remote(self.s1b.at[xs[d]], self.r1b.at[d], xdev[d]) for d in d3]
+            self.two_a = [remote(self.s2a.at[xs[d]], self.r2a.at[d], xdev[d]) for d in d3]
             self.two_b = [remote(self.s2b.at[zs[d]], self.r2b.at[d], zdev[d]) for d in d3]
-            self.three = [remote(self.s3.at[xs[d]], self.r3.at[d], xdev[d]) for d in d3]
+            self.three = [remote(self.s3.at[ys[d]], self.r3.at[d], ydev[d]) for d in d3]
 
         def put(self, lo, grad):
             grad_scale = 1.0 / math.sqrt(CELLS * 128)
@@ -217,6 +217,10 @@
             one, two = grad[:, 0], grad[:, 1]
             self.gw[:, :, lo : lo + 256] = jnp.where(core == 0, one, two)
             self.s0[:, :, lo : lo + 256] = jnp.where(core == 0, two, one).astype(BF16)
+
+        def by_x(self, low, high):
+            pick = lambda t, n: [t[4 * n : 4 * n + 4], t[16 + 4 * n : 20 + 4 * n]]
+            return [jnp.concatenate(pick(low, n) + pick(high, n), 0) for n in range(4)]
 
         def step1(self):
             self.cores[0].wait()
@@ -227,31 +231,32 @@
             for copy in self.one_a:
                 copy.start()
             self.cores[1].wait()
-            for k in range(8):
-                total = self.gw[k, :, self.right] + self.r0[k, :, self.right].astype(F32)
-                self.gw[k, :, self.right] = total
-                low = total.astype(BF16)
-                for h in range(2):
-                    self.s1b[k % 2, h, k // 2] = low[16 * h : 16 * h + 16]
+            for k in range(4):
+                total = self.gw[2 * k : 2 * k + 2, :, self.right]
+                total = total + self.r0[2 * k : 2 * k + 2, :, self.right].astype(F32)
+                for n, rows in enumerate(self.by_x(total[0], total[1])):
+                    self.own_b[n, k] = rows
+                    self.s1b[n, k] = rows.astype(BF16)
             for copy in self.one_b:
                 copy.start()
 
         def step2(self):
             for copy in self.one_a:
                 copy.wait()
+            both = []
             for k in range(2):
                 total = self.gw[z * 2 + k, :, self.left]
                 for d in range(3):
                     total = total + self.r1a[d, k].astype(F32)
-                for h in range(2):
-                    self.s2a[k, h] = total[16 * h : 16 * h + 16]
+                both.append(total)
+            for n, rows in enumerate(self.by_x(*both)):
+                self.s2a[n] = rows
             for copy in self.two_a:
                 copy.start()
             for copy in self.one_b:
                 copy.wait()
-            mine = pl.ds(pl.multiple_of(yh * 16, 16), 16)
             for k in range(4):
-                total = self.gw[k * 2 + yl, mine, self.right]
+                total = self.own_b[x, k]
                 for d in range(3):
                     total = total + self.r1b[d, k].astype(F32)
                 self.s2b[k] = total
@@ -261,20 +266,20 @@
         def step3(self):
             for copy in self.two_a + self.two_b:
                 copy.wait()
-            left, right = self.s2a[yl, yh], self.s2b[z]
+            left, right = self.s2a[x], self.s2b[z]
             for d in range(3):
                 left = left + self.r2a[d]
                 right = right + self.r2b[d]
             for k in range(4):
-                self.s3[k, 0:4, :] = left[4 * k : 4 * k + 4]
-                self.s3[k, 4:8, :] = right[4 * k : 4 * k + 4]
+                self.s3[k // 2, k % 2, 0:4, :] = left[4 * k : 4 * k + 4]
+                self.s3[k // 2, k % 2, 4:8, :] = right[4 * k : 4 * k + 4]
             for copy in self.three:
                 copy.start()
 
         def result(self):
             for copy in self.three:
                 copy.wait()
-            total = self.s3[x] + self.r3[0] + self.r3[1] + self.r3[2]
+            total = self.s3[yl, yh] + self.r3[0] + self.r3[1] + self.r3[2]
             return jnp.concatenate([total[0:4], total[4:8]], 1)
 
     early, final = Scatter(sums[0], 384), Scatter(sums[1], 640)
@@ -329,8 +334,6 @@
 
     for copy in loads:
         copy.wait()
-    gather(0)
-    gather(1)
     for a in range(2):
         lead = [own[a, 0, 0:384, :]]
         lead += [jnp.concatenate([own[a, 0, 384:720, :], own[a, 1, 0:48, :]], 0)]
@@ -339,10 +342,12 @@
         for n, cells in enumerate(lead):
             small = dot(squeeze[:, : cells.shape[0]], cells).astype(BF16)
             lsend[a, 48 * n : 48 * n + 48, :] = small
-    project(0, 2)
     pl.semaphore_wait(barrier, 16)
     for copy in halo_in:
         copy.start()
+    gather(0)
+    gather(1)
+    project(0, 2)
 
     def receive_columns():
         for copy in halo_in[:2]:
@@ -368,6 +373,14 @@
             early.put(256 * n, dot(hidt[...], dproj[:, 512 * n : 512 * n + 256]))
             if n:
                 early.cores[n - 1].start()
+
+    stores = []
+    for rows in (slice(864, 1728), slice(0, 864)):
+        for a in range(2):
+            n = len(stores)
+            stores.append(
+                pltpu.make_async_copy(res[a].at[rows], by_window.at[a, rows], local.at[n])
+            )
 
     def return_halo():
         for a in range(2):
@@ -382,29 +395,37 @@
                     at += n
         for copy in halo_out:
             copy.start()
+        for copy in stores[:2]:
+            copy.start()
+
+    def after_rows():
+        early.step1()
+        outputs(864)
+        return_halo()
 
     @pl.loop(0, 6)
     def _(part):
-        pl.when(part == 2)(receive_columns)
-        pl.when(part == 4)(receive_rows)
-        pl.when(part == 5)(first_gradients)
-        lo = (part % 2) * 256
-        first = jnp.where(part < 2, 0, jnp.where(part < 4, 6, 9))
-        count = jnp.where(part < 2, 6, 3)
+        pl.when(part == 1)(receive_columns)
+        pl.when(part == 3)(receive_rows)
+        pl.when(part == 4)(first_gradients)
+        pl.when(part == 5)(after_rows)
+        inner = jnp.logical_or(part == 0, part == 5)
+        second = jnp.logical_or(part == 2, part >= 4)
+        lo = jnp.where(second, 256, 0)
+        first = jnp.where(inner, 0, jnp.where(part < 3, 6, 9))
+        count = jnp.where(inner, 6, 3)
         key_side = (lax.broadcasted_iota(jnp.int32, (WIN, 1), 0) % 6) >= 3
         lane = lax.broadcasted_iota(jnp.int32, (1, 256), 1)
         query = jnp.where(lane < 128, lane, 128 + lane % 16)
         differ = key_side != ((query % 6) >= 3)
-        apart = jnp.logical_and(part >= 4, lat == lats - 1)
+        apart = jnp.logical_and(first == 9, lat == lats - 1)
         bias[...] = jnp.where(jnp.logical_and(apart, differ), -1e30, 0.0)
 
         @pl.loop(first, first + count)
         def _(w):
             attend(w, lo, proj, datt, bias, hm, hmf, att, dproj, bufs)
 
-    early.step1()
-    outputs(864)
-    return_halo()
+    early.step2()
     attt[...] = att[...].T
     for n in range(5):
         if n < 3:
@@ -414,18 +435,27 @@
         final.put(256 * n, grad)
         if n in (2, 4):
             final.cores[n // 2 - 1].start()
-    early.step2()
+    early.step3()
     outputs(0)
+    for copy in stores[2:]:
+        copy.start()
     final.step1()
-    early.step3()
     final.step2()
     grads = early.result()
     for n in range(3):
         dqkv[:, 512 * n : 512 * n + 256] = grads[:, 256 * n : 256 * n + 256]
     final.step3()
-
-    for copy in halo_out:
+    for copy in stores + halo_out:
         copy.wait()
+    grads = final.result()
+    for n in range(3):
+        dqkv[:, 512 * n + 256 : 512 * n + 512] = grads[:, 256 * n : 256 * n + 256]
+    dwo[...] = grads[:, 768:1280]
+
+
+def settle(by_window, lonin, latin, dqkv, dwo, place, spread, out, dtok, dqkv_out, dwo_out, own, edge, sem):
+    dqkv_out[...] = dqkv[...]
+    dwo_out[...] = dwo[...]
 
     def with_first(cells, first):
         cells = cells.reshape(-1, 24, D)
@@ -433,37 +463,32 @@
         cells = jnp.concatenate([cells[:, 0:8] + first, cells[:, 8:24]], 1)
         return cells.reshape(-1, D).astype(BF16)
 
-    for a in range(2):
+    stores = []
+    for a, ref in enumerate((out, dtok)):
         rows = dot(spread[:96, :48], latin[a, 192:240, :])
         for level in range(2):
             cells = lonin[a, level].astype(F32)
             edge[a, level] = with_first(cells, rows[48 * level : 48 * level + 48])
+        stores.append(pltpu.make_async_copy(edge.at[a], ref.at[:, 0:144], sem.at[2 * a]))
+        stores[-1].start()
         rows = dot(spread[...], latin[a, 0:192, :])
         for strip in range(3):
             for g, runs in enumerate(groups(strip)):
-                cells = windows_of(a, strip, g)
-                whole = dot(place[...], jnp.concatenate(cells, 0))
+                at = [slot(strip, i) * WIN + g * 48 for i in range(4)]
+                cells = jnp.concatenate([by_window[a, n : n + 48, :] for n in at], 0)
+                whole = dot(place[...], cells)
                 at = 0
                 for lev, c, n in runs:
                     keep = min(n, max(0, 30 - c))
                     if keep:
                         top = (lev * 30 + c) * 8
-                        part = with_first(whole[at * 24 : (at + keep) * 24], rows[top : top + 8 * keep])
+                        part = with_first(
+                            whole[at * 24 : (at + keep) * 24], rows[top : top + 8 * keep]
+                        )
                         own[a, lev, c * 24 : (c + keep) * 24, :] = part
                     at += n
-    stores = []
-    for a, ref in enumerate((out, dtok)):
-        stores.append(
-            pltpu.make_async_copy(own.at[a, :, 0:720], ref.at[:, 144:864], local.at[2 * a])
-        )
-        stores.append(pltpu.make_async_copy(edge.at[a], ref.at[:, 0:144], local.at[2 * a + 1]))
-    for copy in stores:
-        copy.start()
-
-    grads = final.result()
-    for n in range(3):
-        dqkv[:, 512 * n + 256 : 512 * n + 512] = grads[:, 256 * n : 256 * n + 256]
-    dwo[...] = grads[:, 768:1280]
+        stores.append(pltpu.make_async_copy(own.at[a], ref.at[:, 144:864], sem.at[2 * a + 1]))
+        stores[-1].start()
     for copy in stores:
         copy.wait()
 
@@ -475,7 +500,7 @@
     shape = jax.ShapeDtypeStruct
     buf = lambda *dims: pltpu.VMEM(dims, BF16)
     buf32 = lambda *dims: pltpu.VMEM(dims, F32)
-    consts = tables()
+    order, place, squeeze, last, last_t, spread, heads, heads32 = tables()
     copies = 12 + 2 * (2 + 6 + 6 + 3)
 
     def scatter(w):
@@ -485,34 +510,35 @@
             buf(8, 32, 2 * w),
             buf(4, 2, 32, w),
             buf(3, 2, 32, w),
-            buf(2, 2, 4, 16, w),
+            buf(4, 4, 16, w),
             buf(3, 4, 16, w),
-            buf32(2, 2, 16, w),
+            buf32(4, 16, w),
             buf32(3, 16, w),
             buf32(4, 16, w),
             buf32(3, 16, w),
-            buf32(4, 8, w),
+            buf32(2, 2, 8, w),
             buf32(3, 8, w),
+            buf32(4, 4, 16, w),
         ]
 
-    out, dtok, dqkv, dwo = pl.pallas_call(
+    limit = 60 * 2**20
+    parts = pl.pallas_call(
         kernel,
         out_shape=(
-            shape((2, 864, D), BF16),
-            shape((2, 864, D), BF16),
+            shape((2, CELLS, D), BF16),
+            shape((2, 2, 144, D), BF16),
+            shape((2, 240, D), BF16),
             shape((4, 3 * D), F32),
             shape((4, D), F32),
         ),
-        in_specs=[hbm, hbm] + [vmem] * (3 + len(consts)),
-        out_specs=(hbm, hbm, vmem, vmem),
+        in_specs=[hbm, hbm] + [vmem] * 10,
+        out_specs=(hbm, hbm, hbm, vmem, vmem),
         scratch_shapes=[
             buf(2, 2, 864, D),
             buf(2, 2, 144, D),
             buf(2, 240, D),
             buf(2, 240, D),
             buf(2, 2, 288, D),
-            buf(2, 240, D),
-            buf(2, 2, 144, D),
             buf(2, 240, D),
             buf(CELLS, D),
             buf(CELLS, D),
@@ -538,7 +564,7 @@
             pltpu.SemaphoreType.DMA((copies,)),
         ],
         compiler_params=pltpu.CompilerParams(
-            collective_id=0, has_side_effects=True, vmem_limit_bytes=60 * 2**20
+            collective_id=0, has_side_effects=True, vmem_limit_bytes=limit
         ),
         name="block",
     )(
@@ -547,8 +573,32 @@
         gain.reshape(1, D),
         qkv_weight,
         out_weight,
-        *consts,
+        order,
+        place,
+        squeeze,
+        last,
+        last_t,
+        heads,
+        heads32,
     )
+    out, dtok, dqkv, dwo = pl.pallas_call(
+        settle,
+        out_shape=(
+            shape((2, 864, D), BF16),
+            shape((2, 864, D), BF16),
+            shape((4, 3 * D), F32),
+            shape((4, D), F32),
+        ),
+        in_specs=[vmem] * 7,
+        out_specs=(hbm, hbm, vmem, vmem),
+        scratch_shapes=[
+            buf(2, 2, 720, D),
+            buf(2, 2, 144, D),
+            pltpu.SemaphoreType.DMA((4,)),
+        ],
+        compiler_params=pltpu.CompilerParams(vmem_limit_bytes=limit),
+        name="settle",
+    )(*parts, place, spread)
     in_place = lambda a: a.reshape(2, 36, 24, D).transpose(0, 2, 1, 3)
     return in_place(out), in_place(dtok), dqkv, dwo
 

time: 91.2 us -> 90.2 us (0.989)
  local copies, waits for them, and re-layouts: 5.36 us -> 0 us
  Pallas kernels: 85.1 us -> 89.2 us
    unnamed x10 -> x0, local copies, waits for them, and re-layouts: 5.36 us -> none
    pallas_call x1 -> x2, Pallas kernels: 85.1 us -> 89.2 us  [the longest x1 83.6 us: per_device(): pl.pallas_call(kernel, out_shape=(shape((2, CELLS, D), BF16), shape((2, 2...]
where the time goes in v4:
time: 90.2 us; the launch traced here: 89.8 us
  Pallas kernels  89.2 us (99%)
    pallas_call x1, Pallas kernels, per_device(): pl.pallas_call(kernel, out_shape=(shape((2, CELLS, D), BF16), shape((2, 2...  83.6 us
    pallas_call x1, Pallas kernels, per_device(): pl.pallas_call(settle, out_shape=(shape((2, 864, D), BF16), shape((2, 864...  5.53 us

profile of v4, /device:TPU:1, one launch (start us, length us, event | category | flops | bytes accessed | tf_op | source)
XLA Modules:
  0.0 89.8 jit_solution(5500898080189357169)
XLA Ops:
  0.6 83.6 %block.1 = (bf16[2,1728,512]{2,1,0:T(8,128)(2,1)}, bf16[2,2,144,512]{3,2,1,0:T(8,128)(2,1)}, bf16[2,240,512]{2,1,0:T(8,128)(2,1)}, f32[4,1536]{1,0:T(4,128)}, f32[4,512]{1,0:T(4,128)}) custom-call(bf16[2,864,512]{2,1,0:T(8,128)(2,1)} %bitcast.13, bf16[2,864,512]{2,1,0:T(8,128)(2,1)} %bitcast.14, f32[1,512]{1,0:T(1,128)} %bitcast.15, bf16[512,1536]{1,0:T(8,128)(2,1)} %wqkv.1, ...), custom_call_target="tpu_custom_call" | custom-call | tf_op jit(solution)/shard_map/block/pallas_call | solution.py:525
  84.3 5.5 %settle.1 = (bf16[2,864,512]{2,1,0:T(8,128)(2,1)}, bf16[2,864,512]{2,1,0:T(8,128)(2,1)}, f32[4,1536]{1,0:T(4,128)}, f32[4,512]{1,0:T(4,128)}) custom-call(bf16[2,1728,512]{2,1,0:T(8,128)(2,1)} %get-tuple-element.13.by_window, bf16[2,2,144,512]{3,2,1,0:T(8,128)(2,1)} %get-tuple-element.14.lonin, bf16[2,240,512]{2,1,0:T(8,128)(2,1)} %get-tuple-element.15.latin, ...), custom_call_target="tpu_custom_call" | custom-call | tf_op jit(solution)/shard_map/settle/pallas_call | solution.py:584

commit v5 on v4

--- a/solution.py
+++ b/solution.py
@@ -131,14 +131,14 @@
 
 
 def kernel(
-    tok, cot, gain, wqkv, wo, order, place, squeeze, late, late_t, hm, hmf,
-    by_window, lonin, latin, dqkv, dwo,
-    own, edge, halo, lsend, region, lout,
+    tok, cot, gain, wqkv, wo, order, place, squeeze, late, late_t, spread, hm, hmf,
+    out, dtok, dqkv, dwo,
+    own, edge, halo, lsend, region, lout, lonin, latin,
     tw, cw, hid, hidt, attt, inv, mean, proj, datt, att, dproj, bias, *more,
 ):
     bufs, more = more[:12], more[12:]
-    sums = (more[:14], more[14:28])
-    local, send, recv = more[28:]
+    sums = (more[:16], more[16:32])
+    local, send, recv = more[32:]
     lon, lat = lax.axis_index("lon"), lax.axis_index("lat")
     lons, lats = lax.axis_size("lon"), lax.axis_size("lat")
     z, yl, core = lon // 4, (lon // 2) % 2, lon % 2
@@ -184,8 +184,8 @@
         )
 
     halo_in, halo_out = [], []
-    for a, ref in enumerate((tok, cot)):
-        halo_in.append(remote(ref.at[:, 0:144], own.at[a, :, 720:864], dev(west, lat)))
+    for a in range(2):
+        halo_in.append(remote(edge.at[a], own.at[a, :, 720:864], dev(west, lat)))
         halo_out.append(remote(region.at[a, :, 144:288], lonin.at[a], dev(east, lat)))
     for a in range(2):
         for rows, lon_in, lon_out in ((slice(0, 192), lon, lon), (slice(192, 240), west, east)):
@@ -198,7 +198,8 @@
     class Scatter:
         def __init__(self, refs, w):
             (self.gw, self.s0, self.r0, self.s1a, self.r1a, self.s1b, self.r1b,
-             self.s2a, self.r2a, self.s2b, self.r2b, self.s3, self.r3, self.own_b) = refs
+             self.s2a, self.r2a, self.s2b, self.r2b, self.s3, self.r3,
+             self.own_b, self.own_a, self.own_c) = refs
             self.left, self.right = slice(0, w), slice(w, 2 * w)
             self.cores = [
                 remote(self.s0.at[:, :, c], self.r0.at[:, :, c], twin)
@@ -222,7 +223,7 @@
             pick = lambda t, n: [t[4 * n : 4 * n + 4], t[16 + 4 * n : 20 + 4 * n]]
             return [jnp.concatenate(pick(low, n) + pick(high, n), 0) for n in range(4)]
 
-        def step1(self):
+        def step1a(self):
             self.cores[0].wait()
             for k in range(8):
                 total = self.gw[k, :, self.left] + self.r0[k, :, self.left].astype(F32)
@@ -230,6 +231,8 @@
                 self.s1a[k // 2, k % 2] = total.astype(BF16)
             for copy in self.one_a:
                 copy.start()
+
+        def step1b(self):
             self.cores[1].wait()
             for k in range(4):
                 total = self.gw[2 * k : 2 * k + 2, :, self.right]
@@ -250,7 +253,8 @@
                     total = total + self.r1a[d, k].astype(F32)
                 both.append(total)
             for n, rows in enumerate(self.by_x(*both)):
-                self.s2a[n] = rows
+                self.own_a[n] = rows
+                self.s2a[n] = rows.astype(BF16)
             for copy in self.two_a:
                 copy.start()
             for copy in self.one_b:
@@ -259,17 +263,18 @@
                 total = self.own_b[x, k]
                 for d in range(3):
                     total = total + self.r1b[d, k].astype(F32)
-                self.s2b[k] = total
+                self.own_c[k] = total
+                self.s2b[k] = total.astype(BF16)
             for copy in self.two_b:
                 copy.start()
 
         def step3(self):
             for copy in self.two_a + self.two_b:
                 copy.wait()
-            left, right = self.s2a[x], self.s2b[z]
+            left, right = self.own_a[x], self.own_c[z]
             for d in range(3):
-                left = left + self.r2a[d]
-                right = right + self.r2b[d]
+                left = left + self.r2a[d].astype(F32)
+                right = right + self.r2b[d].astype(F32)
             for k in range(4):
                 self.s3[k // 2, k % 2, 0:4, :] = left[4 * k : 4 * k + 4]
                 self.s3[k // 2, k % 2, 4:8, :] = right[4 * k : 4 * k + 4]
@@ -315,8 +320,8 @@
 
     res = (hid, datt)
 
-    def outputs(first):
-        @pl.loop(0, 2)
+    def outputs(first, chunks):
+        @pl.loop(0, chunks)
         def _(t):
             rows = pl.ds(pl.multiple_of(first + t * 432, 16), 432)
             cells = tw[rows, :].astype(F32)
@@ -374,14 +379,6 @@
             if n:
                 early.cores[n - 1].start()
 
-    stores = []
-    for rows in (slice(864, 1728), slice(0, 864)):
-        for a in range(2):
-            n = len(stores)
-            stores.append(
-                pltpu.make_async_copy(res[a].at[rows], by_window.at[a, rows], local.at[n])
-            )
-
     def return_halo():
         for a in range(2):
             lout[a] = dot(late_t[...], res[a][1296:1728, :]).astype(BF16)
@@ -395,25 +392,22 @@
                     at += n
         for copy in halo_out:
             copy.start()
-        for copy in stores[:2]:
-            copy.start()
-
     def after_rows():
-        early.step1()
-        outputs(864)
+        early.step1a()
+        early.step1b()
+        outputs(864, 2)
         return_halo()
 
-    @pl.loop(0, 6)
+    @pl.loop(0, 7)
     def _(part):
-        pl.when(part == 1)(receive_columns)
-        pl.when(part == 3)(receive_rows)
-        pl.when(part == 4)(first_gradients)
-        pl.when(part == 5)(after_rows)
-        inner = jnp.logical_or(part == 0, part == 5)
-        second = jnp.logical_or(part == 2, part >= 4)
-        lo = jnp.where(second, 256, 0)
-        first = jnp.where(inner, 0, jnp.where(part < 3, 6, 9))
-        count = jnp.where(inner, 6, 3)
+        pl.when(part == 2)(receive_columns)
+        pl.when(part == 4)(receive_rows)
+        pl.when(part == 5)(first_gradients)
+        pl.when(part == 6)(after_rows)
+        pick = lambda values: sum(jnp.where(part == n, v, 0) for n, v in enumerate(values) if v)
+        lo = pick((0, 256, 0, 256, 0, 256, 256))
+        first = pick((0, 0, 6, 6, 9, 9, 4))
+        count = pick((6, 4, 3, 3, 3, 3, 2))
         key_side = (lax.broadcasted_iota(jnp.int32, (WIN, 1), 0) % 6) >= 3
         lane = lax.broadcasted_iota(jnp.int32, (1, 256), 1)
         query = jnp.where(lane < 128, lane, 128 + lane % 16)
@@ -425,7 +419,6 @@
         def _(w):
             attend(w, lo, proj, datt, bias, hm, hmf, att, dproj, bufs)
 
-    early.step2()
     attt[...] = att[...].T
     for n in range(5):
         if n < 3:
@@ -435,27 +428,20 @@
         final.put(256 * n, grad)
         if n in (2, 4):
             final.cores[n // 2 - 1].start()
+    early.step2()
+    final.step1a()
+    outputs(0, 1)
+    final.step1b()
     early.step3()
-    outputs(0)
-    for copy in stores[2:]:
-        copy.start()
-    final.step1()
+    outputs(432, 1)
     final.step2()
     grads = early.result()
     for n in range(3):
         dqkv[:, 512 * n : 512 * n + 256] = grads[:, 256 * n : 256 * n + 256]
     final.step3()
-    for copy in stores + halo_out:
+
+    for copy in halo_out:
         copy.wait()
-    grads = final.result()
-    for n in range(3):
-        dqkv[:, 512 * n + 256 : 512 * n + 512] = grads[:, 256 * n : 256 * n + 256]
-    dwo[...] = grads[:, 768:1280]
-
-
-def settle(by_window, lonin, latin, dqkv, dwo, place, spread, out, dtok, dqkv_out, dwo_out, own, edge, sem):
-    dqkv_out[...] = dqkv[...]
-    dwo_out[...] = dwo[...]
 
     def with_first(cells, first):
         cells = cells.reshape(-1, 24, D)
@@ -463,20 +449,16 @@
         cells = jnp.concatenate([cells[:, 0:8] + first, cells[:, 8:24]], 1)
         return cells.reshape(-1, D).astype(BF16)
 
-    stores = []
-    for a, ref in enumerate((out, dtok)):
+    for a, settled in enumerate((out, dtok)):
         rows = dot(spread[:96, :48], latin[a, 192:240, :])
         for level in range(2):
             cells = lonin[a, level].astype(F32)
-            edge[a, level] = with_first(cells, rows[48 * level : 48 * level + 48])
-        stores.append(pltpu.make_async_copy(edge.at[a], ref.at[:, 0:144], sem.at[2 * a]))
-        stores[-1].start()
+            settled[level, 0:144, :] = with_first(cells, rows[48 * level : 48 * level + 48])
         rows = dot(spread[...], latin[a, 0:192, :])
         for strip in range(3):
             for g, runs in enumerate(groups(strip)):
-                at = [slot(strip, i) * WIN + g * 48 for i in range(4)]
-                cells = jnp.concatenate([by_window[a, n : n + 48, :] for n in at], 0)
-                whole = dot(place[...], cells)
+                cells = windows_of(a, strip, g)
+                whole = dot(place[...], jnp.concatenate(cells, 0))
                 at = 0
                 for lev, c, n in runs:
                     keep = min(n, max(0, 30 - c))
@@ -485,19 +467,19 @@
                         part = with_first(
                             whole[at * 24 : (at + keep) * 24], rows[top : top + 8 * keep]
                         )
-                        own[a, lev, c * 24 : (c + keep) * 24, :] = part
+                        settled[lev, 144 + c * 24 : 144 + (c + keep) * 24, :] = part
                     at += n
-        stores.append(pltpu.make_async_copy(own.at[a], ref.at[:, 144:864], sem.at[2 * a + 1]))
-        stores[-1].start()
-    for copy in stores:
-        copy.wait()
+
+    grads = final.result()
+    for n in range(3):
+        dqkv[:, 512 * n + 256 : 512 * n + 512] = grads[:, 256 * n : 256 * n + 256]
+    dwo[...] = grads[:, 768:1280]
 
 
 def per_device(tokens, gain, qkv_weight, out_weight, cotangent):
     by_column = lambda a: a.transpose(0, 2, 1, 3).reshape(2, 864, D)
     vmem = pl.BlockSpec(memory_space=pltpu.VMEM)
     hbm = pl.BlockSpec(memory_space=pl.ANY)
-    shape = jax.ShapeDtypeStruct
     buf = lambda *dims: pltpu.VMEM(dims, BF16)
     buf32 = lambda *dims: pltpu.VMEM(dims, F32)
     order, place, squeeze, last, last_t, spread, heads, heads32 = tables()
@@ -512,33 +494,36 @@
             buf(3, 2, 32, w),
             buf(4, 4, 16, w),
             buf(3, 4, 16, w),
-            buf32(4, 16, w),
-            buf32(3, 16, w),
-            buf32(4, 16, w),
-            buf32(3, 16, w),
+            buf(4, 16, w),
+            buf(3, 16, w),
+            buf(4, 16, w),
+            buf(3, 16, w),
             buf32(2, 2, 8, w),
             buf32(3, 8, w),
             buf32(4, 4, 16, w),
+            buf32(4, 16, w),
+            buf32(4, 16, w),
         ]
 
     limit = 60 * 2**20
-    parts = pl.pallas_call(
+    out, dtok, dqkv, dwo = pl.pallas_call(
         kernel,
         out_shape=(
-            shape((2, CELLS, D), BF16),
-            shape((2, 2, 144, D), BF16),
-            shape((2, 240, D), BF16),
-            shape((4, 3 * D), F32),
-            shape((4, D), F32),
+            pltpu.VMEM((2, 864, D), BF16),
+            pltpu.VMEM((2, 864, D), BF16),
+            pltpu.VMEM((4, 3 * D), F32),
+            pltpu.VMEM((4, D), F32),
         ),
-        in_specs=[hbm, hbm] + [vmem] * 10,
-        out_specs=(hbm, hbm, hbm, vmem, vmem),
+        in_specs=[hbm, hbm] + [vmem] * 11,
+        out_specs=(vmem,) * 4,
         scratch_shapes=[
             buf(2, 2, 864, D),
             buf(2, 2, 144, D),
             buf(2, 240, D),
             buf(2, 240, D),
             buf(2, 2, 288, D),
+            buf(2, 240, D),
+            buf(2, 2, 144, D),
             buf(2, 240, D),
             buf(CELLS, D),
             buf(CELLS, D),
@@ -578,27 +563,10 @@
         squeeze,
         last,
         last_t,
+        spread,
         heads,
         heads32,
     )
-    out, dtok, dqkv, dwo = pl.pallas_call(
-        settle,
-        out_shape=(
-            shape((2, 864, D), BF16),
-            shape((2, 864, D), BF16),
-            shape((4, 3 * D), F32),
-            shape((4, D), F32),
-        ),
-        in_specs=[vmem] * 7,
-        out_specs=(hbm, hbm, vmem, vmem),
-        scratch_shapes=[
-            buf(2, 2, 720, D),
-            buf(2, 2, 144, D),
-            pltpu.SemaphoreType.DMA((4,)),
-        ],
-        compiler_params=pltpu.CompilerParams(vmem_limit_bytes=limit),
-        name="settle",
-    )(*parts, place, spread)
     in_place = lambda a: a.reshape(2, 36, 24, D).transpose(0, 2, 1, 3)
     return in_place(out), in_place(dtok), dqkv, dwo
 

time: 90.2 us -> 82.4 us (0.914)
  Pallas kernels: 89.2 us -> 78 us
  local copies, waits for them, and re-layouts: 0 us -> 3.62 us
    pallas_call x2 -> x1, Pallas kernels: 89.2 us -> 78 us  [per_device(): pl.pallas_call(kernel, out_shape=(pltpu.VMEM((2, 864, D), BF16), pltpu.VM...]
    unnamed x0 -> x4, local copies, waits for them, and re-layouts: none -> 3.62 us
where the time goes in v5:
time: 82.4 us; the launch traced here: 82.3 us
  Pallas kernels  78 us (95%)
  local copies, waits for them, and re-layouts  3.62 us (4%)
    pallas_call x1, Pallas kernels, per_device(): pl.pallas_call(kernel, out_shape=(pltpu.VMEM((2, 864, D), BF16), pltpu.VM...  78 us
    unnamed x4, local copies, waits for them, and re-layouts  3.62 us

profile of v5, /device:TPU:1, one launch (start us, length us, event | category | flops | bytes accessed | tf_op | source)
XLA Modules:
  0.0 82.3 jit_solution(1548869669430845595)
XLA Ops:
  0.6 78.0 %block.1 = (bf16[2,864,512]{2,1,0:T(8,128)(2,1)S(1)}, bf16[2,864,512]{2,1,0:T(8,128)(2,1)S(1)}, f32[4,1536]{1,0:T(4,128)S(1)}, f32[4,512]{1,0:T(4,128)S(1)}) custom-call(bf16[2,864,512]{2,1,0:T(8,128)(2,1)} %bitcast.15, bf16[2,864,512]{2,1,0:T(8,128)(2,1)} %bitcast.16, f32[1,512]{1,0:T(1,128)} %bitcast.17, bf16[512,1536]{1,0:T(8,128)(2,1)} %wqkv.1, ...), custom_call_target="tpu_custom_call" | custom-call | tf_op jit(solution)/shard_map/block/pallas_call | solution.py:509
  78.6 1.2 %copy.21 = bf16[2,24,36,512]{3,1,2,0:T(8,128)(2,1)} copy(bf16[2,24,36,512]{3,1,2,0:T(8,128)(2,1)S(1)} %bitcast.14) | data formatting | bytes 3538944
  79.9 1.2 %copy.22 = bf16[2,24,36,512]{3,1,2,0:T(8,128)(2,1)} copy(bf16[2,24,36,512]{3,1,2,0:T(8,128)(2,1)S(1)} %bitcast.13) | data formatting | bytes 3538944
  81.1 0.6 copy.24
  81.7 0.6 copy.23

commit v6 on v5

--- a/solution.py
+++ b/solution.py
@@ -78,13 +78,6 @@
     ref[1024:1152, :] = masked_tail(x, hm)
 
 
-def diagonal_t(ref, x, hm):
-    turned = x[:128].T
-    for h in range(8):
-        ref[32 * h : 32 * h + 32, 128 * h : 128 * h + 128] = turned[32 * h : 32 * h + 32]
-    ref[:, 1024:1152] = masked_tail(x, hm).T
-
-
 def by_query(dst, src):
     for h in range(8):
         at = slice(128 * h, 128 * h + 128)
@@ -99,30 +92,29 @@
 
 
 def attend(w, lo, proj, datt, bias, hm, hmf, att, dproj, bufs):
-    qt, dt, sc, dw, pt, gt, pq, gq, qd, dd, kd, vd = bufs
+    pt, gt, pq, gq, qd, dd, kd, vd = bufs
     rows = pl.ds(pl.multiple_of(w * WIN, 16), WIN)
     cols = lambda off: pl.ds(pl.multiple_of(off + lo, 256), 256)
     q, k, v = proj[rows, cols(0)], proj[rows, cols(512)], proj[rows, cols(1024)]
     da = datt[rows, cols(0)]
-    diagonal_t(qt, q, hm)
-    diagonal_t(dt, da, hm)
-    sc[...] = dot(k, qt[...])
-    dw[...] = dot(v, dt[...])
-    for c in range(9):
-        at = slice(128 * c, 128 * c + 128)
-        s = sc[:, at] + (bias[:, :128] if c < 8 else bias[:, 128:256])
-        d = dw[:, at]
-        e = jnp.exp2((s - jnp.max(s, 0, keepdims=True)) * SCALE_LOG2E)
-        p = e * (1.0 / jnp.sum(e, 0, keepdims=True))
-        pt[:, at] = p.astype(BF16)
-        gt[:, at] = (p * (d - jnp.sum(p * d, 0, keepdims=True)) * SCALE).astype(BF16)
+    diagonal(qd, q, hm)
     diagonal(dd, da, hm)
+    for c in range(0, 1152, 384):
+        scores = dot(k, qd[c : c + 384, :], NT)
+        d_weights = dot(v, dd[c : c + 384, :], NT)
+        for n in range(0, 384, 128):
+            at = slice(c + n, c + n + 128)
+            s = scores[:, n : n + 128] + (bias[:, :128] if c + n < 1024 else bias[:, 128:256])
+            d = d_weights[:, n : n + 128]
+            e = jnp.exp2((s - jnp.max(s, 0, keepdims=True)) * SCALE_LOG2E)
+            p = e * (1.0 / jnp.sum(e, 0, keepdims=True))
+            pt[:, at] = p.astype(BF16)
+            gt[:, at] = (p * (d - jnp.sum(p * d, 0, keepdims=True)) * SCALE).astype(BF16)
     dproj[rows, cols(1024)] = dot(pt[...], dd[...]).astype(BF16)
     by_query(pq, pt)
     diagonal(vd, v, hm)
     a = jnp.concatenate([dot(pq[...], vd[...]), last_queries(pt, v, hmf)], 0)
     att[rows, cols(0)] = a.astype(BF16)
-    diagonal(qd, q, hm)
     dproj[rows, cols(512)] = dot(gt[...], qd[...]).astype(BF16)
     by_query(gq, gt)
     diagonal(kd, k, hm)
@@ -131,12 +123,13 @@
 
 
 def kernel(
-    tok, cot, gain, wqkv, wo, order, place, squeeze, late, late_t, spread, hm, hmf,
+    tok, cot, gain, hbm_wqkv, hbm_wo, hbm_order, hbm_place, hbm_squeeze, hbm_late, hbm_late_t, hbm_spread, hbm_hm, hbm_hmf,
     out, dtok, dqkv, dwo,
+    wqkv, wo, order, place, squeeze, late, late_t, spread, hm, hmf, extra,
     own, edge, halo, lsend, region, lout, lonin, latin,
     tw, cw, hid, hidt, attt, inv, mean, proj, datt, att, dproj, bias, *more,
 ):
-    bufs, more = more[:12], more[12:]
+    bufs, more = more[:8], more[8:]
     sums = (more[:16], more[16:32])
     local, send, recv = more[32:]
     lon, lat = lax.axis_index("lon"), lax.axis_index("lat")
@@ -163,6 +156,14 @@
         loads.append(pltpu.make_async_copy(ref.at[:, 0:144], edge.at[a], local.at[2 * a + 1]))
     for copy in loads:
         copy.start()
+    tables_in = (hbm_squeeze, hbm_order, hbm_wqkv, hbm_wo, hbm_hm, hbm_hmf, hbm_place, hbm_late, hbm_late_t, hbm_spread)
+    tables_to = (squeeze, order, wqkv, wo, hm, hmf, place, late, late_t, spread)
+    params = [
+        pltpu.make_async_copy(src, dst, extra.at[n])
+        for n, (src, dst) in enumerate(zip(tables_in, tables_to))
+    ]
+    for copy in params:
+        copy.start()
     barrier = pltpu.get_barrier_semaphore()
     halo_devs = [dev(west, lat), dev(lon, south), dev(west, south)]
     halo_devs += [dev(east, lat), dev(lon, north), dev(east, north)]
@@ -192,7 +193,7 @@
             halo_in.append(remote(lsend.at[a, rows], halo.at[a, rows], dev(lon_in, south)))
             halo_out.append(remote(lout.at[a, rows], latin.at[a, rows], dev(lon_out, north)))
 
-    for n in (0, 1, 8, 9, 10, 11):
+    for n in (4, 5, 6, 7):
         bufs[n][...] = jnp.zeros_like(bufs[n])
 
     class Scatter:
@@ -337,7 +338,7 @@
         at = [slot(strip, i) * WIN + g * 48 for i in range(4)]
         return [res[a][n : n + 48, :] for n in at]
 
-    for copy in loads:
+    for copy in loads + params[:1]:
         copy.wait()
     for a in range(2):
         lead = [own[a, 0, 0:384, :]]
@@ -350,6 +351,8 @@
     pl.semaphore_wait(barrier, 16)
     for copy in halo_in:
         copy.start()
+    for copy in params[1:]:
+        copy.wait()
     gather(0)
     gather(1)
     project(0, 2)
@@ -514,9 +517,14 @@
             pltpu.VMEM((4, 3 * D), F32),
             pltpu.VMEM((4, D), F32),
         ),
-        in_specs=[hbm, hbm] + [vmem] * 11,
+        in_specs=[hbm, hbm, vmem] + [hbm] * 10,
         out_specs=(vmem,) * 4,
         scratch_shapes=[
+            buf(D, 3 * D),
+            buf(D, D),
+            *[buf(*t.shape) for t in (order, place, squeeze, last, last_t, spread, heads)],
+            buf32(*heads32.shape),
+            pltpu.SemaphoreType.DMA((10,)),
             buf(2, 2, 864, D),
             buf(2, 2, 144, D),
             buf(2, 240, D),
@@ -537,8 +545,6 @@
             buf(CELLS, D),
             buf(CELLS, 3 * D),
             buf32(WIN, 256),
-            *[buf(256, 1152)] * 2,
-            *[buf32(WIN, 1152)] * 2,
             *[buf(WIN, 1152)] * 2,
             *[buf(128, 1152)] * 2,
             *[buf(1152, 256)] * 4,

time: 82.4 us -> 80.2 us (0.973)
  Pallas kernels: 78 us -> 75.8 us
    pallas_call x1, Pallas kernels: 78 us -> 75.8 us  [per_device(): pl.pallas_call(kernel, out_shape=(pltpu.VMEM((2, 864, D), BF16), pltpu.VM...]
where the time goes in v6:
time: 80.2 us; the launch traced here: 80.1 us
  Pallas kernels  75.8 us (95%)
  local copies, waits for them, and re-layouts  3.62 us (5%)
    pallas_call x1, Pallas kernels, per_device(): pl.pallas_call(kernel, out_shape=(pltpu.VMEM((2, 864, D), BF16), pltpu.VM...  75.8 us
    unnamed x4, local copies, waits for them, and re-layouts  3.62 us

profile of v6, /device:TPU:1, one launch (start us, length us, event | category | flops | bytes accessed | tf_op | source)
XLA Modules:
  0.0 80.1 jit_solution(1910974629504708992)
XLA Ops:
  0.6 75.8 %block.1 = (bf16[2,864,512]{2,1,0:T(8,128)(2,1)S(1)}, bf16[2,864,512]{2,1,0:T(8,128)(2,1)S(1)}, f32[4,1536]{1,0:T(4,128)S(1)}, f32[4,512]{1,0:T(4,128)S(1)}) custom-call(bf16[2,864,512]{2,1,0:T(8,128)(2,1)} %bitcast.15, bf16[2,864,512]{2,1,0:T(8,128)(2,1)} %bitcast.16, f32[1,512]{1,0:T(1,128)} %bitcast.17, bf16[512,1536]{1,0:T(8,128)(2,1)} %hbm_wqkv.1, ...), custom_call_target="tpu_custom_call" | custom-call | tf_op jit(solution)/shard_map/block/pallas_call | solution.py:512
  76.5 1.2 %copy.21 = bf16[2,24,36,512]{3,1,2,0:T(8,128)(2,1)} copy(bf16[2,24,36,512]{3,1,2,0:T(8,128)(2,1)S(1)} %bitcast.14) | data formatting | bytes 3538944
  77.7 1.2 %copy.22 = bf16[2,24,36,512]{3,1,2,0:T(8,128)(2,1)} copy(bf16[2,24,36,512]{3,1,2,0:T(8,128)(2,1)S(1)} %bitcast.13) | data formatting | bytes 3538944
  78.9 0.6 copy.24
  79.5 0.6 copy.23

commit v7 on v6

--- a/solution.py
+++ b/solution.py
@@ -385,6 +385,9 @@
     def return_halo():
         for a in range(2):
             lout[a] = dot(late_t[...], res[a][1296:1728, :]).astype(BF16)
+        for copy in halo_out[2:]:
+            copy.start()
+        for a in range(2):
             for g, runs in enumerate(groups(2)):
                 cells = windows_of(a, 2, g)
                 whole = dot(place[...], jnp.concatenate(cells, 0)).astype(BF16)
@@ -393,7 +396,7 @@
                     to = slice((c - 24) * 24, (c - 24 + n) * 24)
                     region[a, lev, to, :] = whole[at * 24 : (at + n) * 24]
                     at += n
-        for copy in halo_out:
+        for copy in halo_out[:2]:
             copy.start()
     def after_rows():
         early.step1a()
@@ -431,17 +434,17 @@
         final.put(256 * n, grad)
         if n in (2, 4):
             final.cores[n // 2 - 1].start()
+    final.step1a()
     early.step2()
-    final.step1a()
     outputs(0, 1)
     final.step1b()
+    outputs(432, 1)
     early.step3()
-    outputs(432, 1)
     final.step2()
+    final.step3()
     grads = early.result()
     for n in range(3):
         dqkv[:, 512 * n : 512 * n + 256] = grads[:, 256 * n : 256 * n + 256]
-    final.step3()
 
     for copy in halo_out:
         copy.wait()

time: 80.2 us -> 79.7 us (level)
  no operation moved by 1% of the time
where the time goes in v7:
time: 79.7 us; the launch traced here: 79.4 us
  Pallas kernels  75.2 us (94%)
  local copies, waits for them, and re-layouts  3.62 us (5%)
    pallas_call x1, Pallas kernels, per_device(): pl.pallas_call(kernel, out_shape=(pltpu.VMEM((2, 864, D), BF16), pltpu.VM...  75.2 us
    unnamed x4, local copies, waits for them, and re-layouts  3.62 us

profile of v7, /device:TPU:1, one launch (start us, length us, event | category | flops | bytes accessed | tf_op | source)
XLA Modules:
  0.0 79.4 jit_solution(5344827014230455755)
XLA Ops:
  0.6 75.2 %block.1 = (bf16[2,864,512]{2,1,0:T(8,128)(2,1)S(1)}, bf16[2,864,512]{2,1,0:T(8,128)(2,1)S(1)}, f32[4,1536]{1,0:T(4,128)S(1)}, f32[4,512]{1,0:T(4,128)S(1)}) custom-call(bf16[2,864,512]{2,1,0:T(8,128)(2,1)} %bitcast.15, bf16[2,864,512]{2,1,0:T(8,128)(2,1)} %bitcast.16, f32[1,512]{1,0:T(1,128)} %bitcast.17, bf16[512,1536]{1,0:T(8,128)(2,1)} %hbm_wqkv.1, ...), custom_call_target="tpu_custom_call" | custom-call | tf_op jit(solution)/shard_map/block/pallas_call | solution.py:515
  75.8 1.2 %copy.21 = bf16[2,24,36,512]{3,1,2,0:T(8,128)(2,1)} copy(bf16[2,24,36,512]{3,1,2,0:T(8,128)(2,1)S(1)} %bitcast.14) | data formatting | bytes 3538944
  77.0 1.2 %copy.22 = bf16[2,24,36,512]{3,1,2,0:T(8,128)(2,1)} copy(bf16[2,24,36,512]{3,1,2,0:T(8,128)(2,1)S(1)} %bitcast.13) | data formatting | bytes 3538944
  78.2 0.6 copy.24
  78.8 0.6 copy.23
